TPU v7x, 32 devices: a whole 2x2x4 slice. The times are simulated.
32 devices in a mesh: groups: 2 (over x), pool: 8 (over z, y), tp: 2 (over core).
Axes of the slice: x: 2, y: 2, z: 4, core: 2. Of those that a mesh axis runs over, the one named last changes fastest.
Arguments:
- q_lat: bfloat16 [2048, 64, 512], P(('groups', 'pool'), 'tp'), parts along dimension 0, may hold values from -8 to 8
- q_rope: bfloat16 [2048, 4096], P(('groups', 'pool'), 'tp'), parts along dimension 0, may hold values from -80 to 80
- new_lat: bfloat16 [2048, 512], P(('groups', 'pool')), parts along dimension 0, may hold values from -6 to 6
- new_rope: bfloat16 [2048, 64], P(('groups', 'pool')), parts along dimension 0, may hold values from -24 to 24
- pool_lat: bfloat16 [256, 64, 512], P(('groups', 'pool')), parts along dimension 0, may hold values from -6 to 6
- pool_rope: bfloat16 [256, 4096], P(('groups', 'pool')), parts along dimension 0, may hold values from -6 to 6
- hit_block: int32 [96], P(('groups', 'pool')), parts along dimension 0, may hold values from 0 to 15
- hit_owner: int32 [96, 1], P(('groups', 'pool')), parts along dimension 0, may hold values from 0 to 7; in each aligned block of 6 rows (0 to 5, 6 to 11, ...) at most 2 rows name the same one
- suffix_len: int32 [16], P(('groups', 'pool')), parts along dimension 0, may hold values from 1 to 128, 768 in all
- new_place: int32 [32], P(('groups', 'pool')), parts along dimension 0, may hold values from 0 to 15, each once
- w_uv: bfloat16 [64, 512, 128], P('tp'), may hold values from -0.5 to 0.5
Outputs:
- attn_out: bfloat16 [2048, 8192], P(('groups', 'pool'), 'tp'), parts along dimension 0
- written_lat: bfloat16 [32, 64, 512], P(('groups', 'pool')), parts along dimension 0
- written_rope: bfloat16 [32, 4096], P(('groups', 'pool')), parts along dimension 0
There are 2 independent parts, one for each index of `groups`. A program takes and returns all parts, laid end to end along the dimension named above; an argument that names none is the same for every part. Nothing has to cross between parts.
Inputs may be any that keep to these rules, and one draw needn't show every extreme that they name: `hit_owner`: among the 6 hits of one request no owner is named more than 2 times, a bound that some block reaches. `suffix_len`: some request of a group has exactly 128 live tokens. `new_place`: every new block is named exactly once.
All inputs are finite; a program needn't handle non-finite values.
Results may differ from a plain program's by a relative error of at most 0.0058.
Values may be sent and summed in bfloat16 or wider, within the bound.
No kernel may reach another device: no remote copies, remote signals or barrier semaphores. Data moves between devices by JAX's collectives and lax.ppermute only.
A program may use at most 128 MiB of HBM per device.

v0:
```python
import math

import jax
import jax.numpy as jnp
from jax import lax
from jax.sharding import PartitionSpec as P

CAP = 2


softmax_scale = 1.0 / math.sqrt(192.0)


def slot_ranks(owners):
    hit_count = owners.shape[-1]
    positions = lax.iota(jnp.int32, hit_count)
    same_owner = owners[..., :, None] == owners[..., None, :]
    before = positions[None, :] < positions[:, None]
    return jnp.sum((same_owner & before).astype(jnp.int32), axis=-1)


def local(
    q_lat,
    q_rope,
    new_lat,
    new_rope,
    pool_lat,
    pool_rope,
    hit_block,
    hit_owner,
    suffix_len,
    new_place,
    w_uv,
):
    pool_count = lax.axis_size("pool")
    hit_count = hit_block.shape[0]
    owners = hit_owner[:, 0]
    slots = owners * CAP + slot_ranks(owners)
    slot_ids = lax.iota(jnp.int32, pool_count * CAP)
    request_ids = jnp.sum(
        jnp.where(slots[None, :] == slot_ids[:, None], hit_block[None, :], 0), axis=1
    )
    request_ids = request_ids.reshape(pool_count, CAP)
    block_ids = lax.all_to_all(request_ids, "pool", split_axis=0, concat_axis=0, tiled=True)
    found_lat = pool_lat[block_ids]
    found_rope = pool_rope[block_ids]
    got_lat = lax.all_to_all(found_lat, "pool", split_axis=0, concat_axis=0, tiled=True)
    got_rope = lax.all_to_all(found_rope, "pool", split_axis=0, concat_axis=0, tiled=True)
    block_len = pool_lat.shape[1]
    latent_width = pool_lat.shape[2]
    rope_width = new_rope.shape[1]
    prefix_len = hit_count * block_len
    prefix_lat = got_lat.reshape(pool_count * CAP, block_len, latent_width)[slots].reshape(
        prefix_len, latent_width
    )
    prefix_rope = got_rope.reshape(pool_count * CAP, block_len * rope_width)[slots].reshape(
        prefix_len, rope_width
    )
    suffix_rows = new_lat.shape[0]
    length = suffix_len[0]
    positions = lax.iota(jnp.int32, suffix_rows)
    live_rows = positions < length
    new_count = suffix_rows // block_len
    masked_lat = jnp.where(live_rows[:, None], new_lat, jnp.zeros_like(new_lat)).reshape(
        new_count, block_len, latent_width
    )
    masked_rope = jnp.where(live_rows[:, None], new_rope, jnp.zeros_like(new_rope)).reshape(
        new_count, block_len * rope_width
    )
    every_lat, every_rope = (
        lax.all_gather(masked_lat, "pool", axis=0, tiled=True),
        lax.all_gather(masked_rope, "pool", axis=0, tiled=True),
    )
    written_lat = every_lat[new_place]
    written_rope = every_rope[new_place]
    heads_local = q_lat.shape[1]
    query_rope = q_rope.reshape(suffix_rows, heads_local, rope_width)
    keys_lat = jnp.concatenate([prefix_lat, new_lat], axis=0)
    keys_rope = jnp.concatenate([prefix_rope, new_rope], axis=0)
    scores = jnp.einsum("shl,kl->shk", q_lat, keys_lat, preferred_element_type=jnp.float32)
    scores = scores + jnp.einsum(
        "shr,kr->shk", query_rope, keys_rope, preferred_element_type=jnp.float32
    )
    scores = scores * softmax_scale
    key_pos = lax.iota(jnp.int32, prefix_len + suffix_rows)
    allowed = (key_pos[None, :] < prefix_len) | (
        key_pos[None, :] - prefix_len <= positions[:, None]
    )
    scores = jnp.where(allowed[:, None, :], scores, -1e30)
    weights = jax.nn.softmax(scores, axis=-1).astype(jnp.bfloat16)
    context = jnp.einsum(
        "shk,kl->shl", weights, keys_lat, preferred_element_type=jnp.float32
    ).astype(jnp.bfloat16)
    result = jnp.einsum("shl,hlv->shv", context, w_uv, preferred_element_type=jnp.float32)
    result = jnp.where(live_rows[:, None, None], result, 0.0)
    attn_out = result.astype(jnp.bfloat16).reshape(suffix_rows, heads_local * w_uv.shape[2])
    return (attn_out, written_lat, written_rope)


def solution(mesh):
    return jax.shard_map(
        local,
        mesh=mesh,
        in_specs=(
            P(("groups", "pool"), "tp", None),
            P(("groups", "pool"), "tp"),
            P(("groups", "pool"), None),
            P(("groups", "pool"), None),
            P(("groups", "pool"), None, None),
            P(("groups", "pool"), None),
            P(("groups", "pool")),
            P(("groups", "pool"), None),
            P(("groups", "pool")),
            P(("groups", "pool")),
            P("tp", None, None),
        ),
        out_specs=(
            P(("groups", "pool"), "tp"),
            P(("groups", "pool"), None, None),
            P(("groups", "pool"), None),
        ),
        check_vma=False,
    )
```

profile of v0, /device:TPU:0, one launch (start us, length us, event | category | flops | bytes accessed | tf_op | source)
XLA Modules:
  0.0 134.2 jit_solution(13575371635829776348)
XLA Ops:
  7.2 0.0 copy-start
  7.2 0.0 copy-start.2
  7.2 0.9 convert_reduce_fusion
  8.1 0.7 multiply_add_fusion
  8.8 0.7 select_reduce_fusion
  9.5 0.7 all_to_all.14
  10.2 7.3 %all-to-all-start = ((s32[8,1,2]{2,1,0:T(1,128)}), s32[8,1,2]{2,1,0:T(1,128)S(1)}, u32[]{:S(2)}, u32[]{:S(2)}) async-start(s32[8,1,2]{2,1,0:T(1,128)} %bitcast.2), calls=%async_computation | async-start | bytes 8192 | tf_op jit(solution)/shard_map/all_to_all | solution.py:44
  18.2 5.7 %all-to-all-done = s32[8,1,2]{2,1,0:T(1,128)S(1)} async-done(((s32[8,1,2]{2,1,0:T(1,128)}), s32[8,1,2]{2,1,0:T(1,128)S(1)}, u32[]{:S(2)}, u32[]{:S(2)}) %all-to-all-start) | async-done | bytes 96 | tf_op jit(solution)/shard_map/all_to_all | solution.py:44
  23.9 0.1 copy.39
  24.0 0.1 copy.40
  24.1 0.1 reshape.132
  24.2 1.7 %gather_fusion.2 = bf16[16,4096]{1,0:T(8,128)(2,1)S(1)} fusion(bf16[16,4096]{1,0:T(8,128)(2,1)} %param.16, s32[1024]{0:T(1024)S(1)} %pad_clamp_fusion.2), kind=kCustom, calls=%fused_computation.2 | custom fusion | bytes 262208 | tf_op jit(solution)/shard_map/gather | solution.py:46
  25.8 0.8 reshape.147
  26.6 3.4 %all-to-all-start.2 = ((bf16[8,2,4096]{2,1,0:T(2,128)(2,1)}), bf16[8,2,4096]{2,1,0:T(2,128)(2,1)S(1)}, u32[]{:S(2)}, u32[]{:S(2)}) async-start(bf16[8,2,4096]{2,1,0:T(2,128)(2,1)} %reshape.147), calls=%async_computation.2 | async-start | bytes 262144 | tf_op jit(solution)/shard_map/all_to_all | solution.py:48
  30.0 0.0 all-gather.3.cloned.1.call-start
  30.0 1.6 %broadcast_select_fusion = bf16[128,512]{1,0:T(8,128)(2,1)} fusion(bf16[128,512]{1,0:T(8,128)(2,1)} %param.13, pred[128]{0:T(512)(128)(4,1)S(1)} %iota_compare_fusion.4), kind=kLoop, calls=%fused_computation.19 | loop fusion | flops 65536 | bytes 262272 | tf_op jit(solution)/shard_map/jit(_where)/select_n | solution.py:64
  31.7 0.0 all-gather.3.cloned.1.call-update
  31.7 0.0 copy-done
  31.7 1.6 %gather_fusion = bf16[16,64,512]{2,1,0:T(8,128)(2,1)} fusion(bf16[16,64,512]{2,1,0:T(8,128)(2,1)S(1)} %copy-done, s32[1024]{0:T(1024)S(1)} %pad_clamp_fusion.2), kind=kCustom, calls=%fused_computation | custom fusion | bytes 2097216 | tf_op jit(solution)/shard_map/gather | solution.py:45
  33.3 4.0 %all-to-all-done.2 = bf16[8,2,4096]{2,1,0:T(2,128)(2,1)S(1)} async-done(((bf16[8,2,4096]{2,1,0:T(2,128)(2,1)}), bf16[8,2,4096]{2,1,0:T(2,128)(2,1)S(1)}, u32[]{:S(2)}, u32[]{:S(2)}) %all-to-all-start.2) | async-done | bytes 131104 | tf_op jit(solution)/shard_map/all_to_all | solution.py:48
  37.3 3.6 %all-to-all-start.1 = ((bf16[8,2,64,512]{3,2,1,0:T(8,128)(2,1)}), bf16[8,2,64,512]{3,2,1,0:T(8,128)(2,1)S(1)}, u32[]{:S(2)}, u32[]{:S(2)}) async-start(bf16[8,2,64,512]{3,2,1,0:T(8,128)(2,1)} %bitcast.4), calls=%async_computation.1 | async-start | bytes 2097152 | tf_op jit(solution)/shard_map/all_to_all | solution.py:47
  40.8 1.3 copy.43
  42.1 0.7 broadcast_select_fusion.1
  42.9 0.1 copy.46
  43.0 0.1 reshape.182
  43.1 49.8 %all-gather = bf16[8,2,4096]{2,1,0:T(2,128)(2,1)S(1)} all-gather(bf16[1,2,4096]{2,1,0:T(2,128)(2,1)S(1)} %reshape.182), channel_id=1, replica_groups=mesh['groups'=2,'pool'=8,'tp'=2] {'pool'}, dimensions={0}, use_global_device_ids=true | all-gather | bytes 147456 | tf_op jit(solution)/shard_map/all_gather | solution.py:72
  92.9 0.1 reshape.183
  93.0 0.7 compare_select_fusion.1
  93.6 1.2 gather_fusion.5
  94.8 0.7 fusion.12
  95.5 0.2 fusion.8
  95.7 0.0 copy-start.3
  95.7 0.1 reshape.124
  95.8 0.6 gather_fusion.3
  96.4 0.1 reshape.125
  96.5 0.1 copy.42
  96.6 0.0 all-gather.3.cloned.1.call-done
  96.6 2.4 %gather_fusion.4 = bf16[2,64,512]{2,1,0:T(8,128)(2,1)} fusion(bf16[16,64,512]{2,1,0:T(8,128)(2,1)} %all-gather.3.cloned.1.call-done, s32[1024]{0:T(1024)S(1)} %pad_clamp_fusion), kind=kCustom, calls=%fused_computation.4 | custom fusion | bytes 262152 | tf_op jit(solution)/shard_map/gather | solution.py:74
  99.0 0.0 all-to-all-done.1
  99.0 0.6 gather_fusion.1
  99.6 0.0 copy-done.2
  99.6 9.0 %fusion.1 = f32[512,128,32]{1,0,2:T(8,128)S(1)} fusion(bf16[128,32,512]{2,1,0:T(8,128)(2,1)} %param.11, bf16[128,512]{1,0:T(8,128)(2,1)S(1)} %copy-done.2, bf16[384,512]{1,0:T(8,128)(2,1)S(1)} %bitcast.39), kind=kOutput, calls=%fused_computation.10 | convolution fusion | flops 2148532224 | bytes 13107200 | tf_op jit(solution)/shard_map/shl,kl->shk/dot_general | solution.py:80
  108.6 0.0 copy-done.3
  108.6 1.5 %bitcast_select_fusion = f32[128,32,512]{0,2,1:T(8,128)S(1)} fusion(f32[512,128,32]{1,0,2:T(8,128)S(1)} %fusion.1, pred[128,512]{0,1:T(8,128)(4,1)S(1)} %fusion.8, bf16[128,32,64]{0,2,1:T(8,128)(2,1)S(1)} %bitcast.37, bf16[128,64]{0,1:T(8,128)(2,1)S(1)} %copy-done.3, bf16[384,64]{0,1:T(8,128)(2,1)S(1)} %copy.42), kind=kOutput, calls=%fused_computation.7 | convolution fusion | flops 274857984 | bytes 17432576 | tf_op jit(solution)/shard_map/shr,kr->shk/dot_general | solution.py:81
  110.1 0.0 copy-start.1
  110.1 3.2 %copy-done.1 = f32[128,32,512]{0,2,1:T(8,128)} copy-done((f32[128,32,512]{0,2,1:T(8,128)}, f32[128,32,512]{0,2,1:T(8,128)S(1)}, u32[]{:S(2)}) %copy-start.1) | copy-done | bytes 8388632
  113.4 1.5 %fusion.19 = f32[128,32]{0,1:T(8,128)S(1)} fusion(f32[128,32,512]{0,2,1:T(8,128)S(1)} %bitcast_select_fusion), kind=kOutput, calls=%fused_computation.45 | output fusion | flops 4194815 | bytes 8404992 | tf_op jit(solution)/shard_map/sub | solution.py:90
  114.9 11.2 %select_convert_fusion = bf16[32,128,128]{1,2,0:T(8,128)(2,1)S(1)} fusion(bf16[32,512,128]{2,1,0:T(8,128)(2,1)} %param.21, f32[128,32]{0,1:T(8,128)S(1)} %fusion.19, pred[128]{0:T(512)(128)(4,1)S(1)} %iota_compare_fusion.4, bf16[128,512]{1,0:T(8,128)(2,1)S(1)} %copy-done.2, bf16[384,512]{1,0:T(8,128)(2,1)S(1)} %bitcast.40, f32[128,32,512]{0,2,1:T(8,128)} %copy-done.1), kind=kOutput, calls=%fused_computation.15 | convolution fusion | flops 2694844928 | bytes 14172288 | tf_op jit(solution)/shard_map/shl,hlv->shv/dot_general | solution.py:94
  126.1 1.3 copy.47
  (7 shorter events, 0.0 us)
Async XLA Ops:
  7.2 24.5 %copy-start = (bf16[16,64,512]{2,1,0:T(8,128)(2,1)S(1)}, bf16[16,64,512]{2,1,0:T(8,128)(2,1)}, u32[]{:S(2)}) copy-start(bf16[16,64,512]{2,1,0:T(8,128)(2,1)} %param.15) | copy-start | bytes 3145732
  7.2 92.4 %copy-start.2 = (bf16[128,512]{1,0:T(8,128)(2,1)S(1)}, bf16[128,512]{1,0:T(8,128)(2,1)}, u32[]{:S(2)}) copy-start(bf16[128,512]{1,0:T(8,128)(2,1)} %param.13) | copy-start | bytes 393220
  10.2 13.7 %all-to-all-start = ((s32[8,1,2]{2,1,0:T(1,128)}), s32[8,1,2]{2,1,0:T(1,128)S(1)}, u32[]{:S(2)}, u32[]{:S(2)}) async-start(s32[8,1,2]{2,1,0:T(1,128)} %bitcast.2), calls=%async_computation | async-start | bytes 8192 | tf_op jit(solution)/shard_map/all_to_all | solution.py:44
  26.6 10.7 %all-to-all-start.2 = ((bf16[8,2,4096]{2,1,0:T(2,128)(2,1)}), bf16[8,2,4096]{2,1,0:T(2,128)(2,1)S(1)}, u32[]{:S(2)}, u32[]{:S(2)}) async-start(bf16[8,2,4096]{2,1,0:T(2,128)(2,1)} %reshape.147), calls=%async_computation.2 | async-start | bytes 262144 | tf_op jit(solution)/shard_map/all_to_all | solution.py:48
  30.0 66.6 %all-gather.3.cloned.1.call-start = ((), (), s32[]{:S(2)}) async-start(), calls=%async_computation.3 | async-start | bytes 1179648 | tf_op jit(solution)/shard_map/all_gather | solution.py:71
  37.3 61.8 %all-to-all-start.1 = ((bf16[8,2,64,512]{3,2,1,0:T(8,128)(2,1)}), bf16[8,2,64,512]{3,2,1,0:T(8,128)(2,1)S(1)}, u32[]{:S(2)}, u32[]{:S(2)}) async-start(bf16[8,2,64,512]{3,2,1,0:T(8,128)(2,1)} %bitcast.4), calls=%async_computation.1 | async-start | bytes 2097152 | tf_op jit(solution)/shard_map/all_to_all | solution.py:47
  95.7 12.9 %copy-start.3 = (bf16[128,64]{0,1:T(8,128)(2,1)S(1)}, bf16[128,64]{0,1:T(8,128)(2,1)}, u32[]{:S(2)}) copy-start(bf16[128,64]{0,1:T(8,128)(2,1)} %param.14) | copy-start | bytes 49156
  110.1 3.2 %copy-start.1 = (f32[128,32,512]{0,2,1:T(8,128)}, f32[128,32,512]{0,2,1:T(8,128)S(1)}, u32[]{:S(2)}) copy-start(f32[128,32,512]{0,2,1:T(8,128)S(1)} %bitcast_select_fusion) | copy-start | bytes 25165828
Sparse Core Ops, SparseCore 0:
  32.9 46.8 all-gather.2
where the time goes:
time: 135 us; the launch traced here: 134 us
  blocking collectives  49.8 us (37%)
  matrix products  21.7 us (16%)
  local copies, waits for them, and re-layouts  16.1 us (12%)
  between operations  14.9 us (11%)
  starting transfers between devices  14.3 us (11%)
  waiting for transfers between devices  9.74 us (7%)
  other arithmetic  7.8 us (6%)
    all_gather x1, blocking collectives, local(): lax.all_gather(masked_rope, 'pool', axis=0, tiled=True)  49.8 us
    dot_general x1, matrix products, local(): jnp.einsum('shl,hlv->shv', context, w_uv, preferred_element_type=jnp.floa...  11.2 us
    dot_general x1, matrix products, local(): jnp.einsum('shl,kl->shk', q_lat, keys_lat, preferred_element_type=jnp.flo...  8.97 us
    all_to_all x1, starting transfers between devices, local(): lax.all_to_all(request_ids, 'pool', split_axis=0, concat_axis=0, tiled=True)  7.28 us
    unnamed x12, local copies, waits for them, and re-layouts  6.03 us
    all_to_all x1, waiting for transfers between devices, local(): lax.all_to_all(request_ids, 'pool', split_axis=0, concat_axis=0, tiled=True)  5.73 us
    all_to_all x1, waiting for transfers between devices, local(): lax.all_to_all(found_rope, 'pool', split_axis=0, concat_axis=0, tiled=True)  3.97 us
    all_to_all x1, starting transfers between devices, local(): lax.all_to_all(found_lat, 'pool', split_axis=0, concat_axis=0, tiled=True)  3.56 us
  transfers between devices with their start and end apart: 4, of which 2 were waited for; matrix products, arithmetic and copies ran while one was open for 9% of the time, Pallas kernels for 0%

commit v1 on v0

v1 whole, which is shorter than its diff:
```python
import functools
import math

import jax
import jax.numpy as jnp
from jax import lax
from jax.experimental import pallas as pl
from jax.experimental.pallas import tpu as pltpu
from jax.sharding import PartitionSpec as P

CAP = 2
LANES = 128
softmax_scale = 1.0 / math.sqrt(192.0)
exp2_scale = softmax_scale / math.log(2.0)


def gather_kernel(hits, asks, pool_ref, out_ref, sem):
    me = lax.axis_index("pool")
    peers = out_ref.shape[0]

    def each_request(fn):
        def body(r, carry):
            rank = jnp.int32(0)
            for k in range(hits):
                mine = asks[r, k] == me

                @pl.when(mine)
                def _(rank=rank, k=k):
                    fn(r, rank, asks[r, hits + k])

                rank = rank + mine.astype(jnp.int32)
            return carry

        lax.fori_loop(0, peers, body, 0)

    def copy(r, rank, block):
        slot = jnp.minimum(rank, CAP - 1)
        return pltpu.make_async_copy(pool_ref.at[block], out_ref.at[r, slot], sem)

    each_request(lambda r, rank, block: copy(r, rank, block).start())
    each_request(lambda r, rank, block: copy(r, rank, block).wait())


def attend_kernel(
    block_len,
    owners,
    length,
    own_ref,
    sib_ref,
    new_lat_ref,
    new_rope_ref,
    q_ref,
    qr_ref,
    w_ref,
    out_ref,
    keys,
    rope,
):
    hits = owners.shape[0]
    group, rows, latent = q_ref.shape
    rope_width = qr_ref.shape[2]
    half = block_len // 2
    quarter = half // 2
    prefix = hits * block_len
    total = prefix + rows
    tiles = latent // LANES

    @pl.when(pl.program_id(0) == 0)
    def _():
        for k in range(hits):
            owner = owners[k]
            rank = jnp.int32(0)
            for j in range(k):
                rank = rank + (owners[j] == owner).astype(jnp.int32)
            for side, ref in enumerate((own_ref, sib_ref)):
                block = ref.at[owner, jnp.minimum(rank, CAP - 1)]
                base = k * block_len + side * half
                for t in range(tiles):
                    keys[base : base + half, t * LANES : (t + 1) * LANES] = block[
                        t * half : (t + 1) * half, :
                    ]
                packed = block[tiles * half : tiles * half + quarter, :]
                rope[base : base + quarter, :] = packed[:, :rope_width]
                rope[base + quarter : base + half, :] = packed[:, rope_width:]
        keys[prefix:, :] = new_lat_ref[...]
        rope[prefix:, :] = new_rope_ref[...]

    contract = (((1,), (1,)), ((), ()))
    q = q_ref[...].reshape(group * rows, latent)
    qr = qr_ref[...].reshape(group * rows, rope_width)
    scores = lax.dot_general(q, keys[...], contract, preferred_element_type=jnp.float32)
    scores = scores + lax.dot_general(
        qr, rope[...], contract, preferred_element_type=jnp.float32
    )
    position = lax.broadcasted_iota(jnp.int32, (group, rows, rows), 1).reshape(group * rows, rows)
    key_at = lax.broadcasted_iota(jnp.int32, (group * rows, rows), 1)
    tail = jnp.where(key_at <= position, scores[:, prefix:], -1e30)
    scores = jnp.concatenate([scores[:, :prefix], tail], axis=1)
    top = jnp.max(scores, axis=1, keepdims=True)
    parts = jnp.exp2((scores - top) * exp2_scale)
    norm = 1.0 / jnp.sum(parts, axis=1, keepdims=True)
    weights = (parts * norm).astype(jnp.bfloat16)
    context = jnp.dot(weights, keys[...], preferred_element_type=jnp.float32).astype(jnp.bfloat16)
    width = w_ref.shape[2]
    live = lax.broadcasted_iota(jnp.int32, (rows, width), 0) < length[0]
    for g in range(group):
        result = jnp.dot(
            context[g * rows : (g + 1) * rows], w_ref[g], preferred_element_type=jnp.float32
        )
        out_ref[:, g * width : (g + 1) * width] = jnp.where(live, result, 0.0).astype(
            out_ref.dtype
        )


def local(
    q_lat,
    q_rope,
    new_lat,
    new_rope,
    pool_lat,
    pool_rope,
    hit_block,
    hit_owner,
    suffix_len,
    new_place,
    w_uv,
):
    peers = lax.axis_size("pool")
    me = lax.axis_index("pool")
    core = lax.axis_index("tp")
    cores = lax.axis_size("tp")
    assert cores == 2
    hits = hit_block.shape[0]
    blocks, block_len, latent = pool_lat.shape
    rows, rope_width = new_rope.shape
    half = block_len // 2
    quarter = half // 2
    tiles = latent // LANES
    heads = q_lat.shape[1]
    vhead = w_uv.shape[2]
    new_count = rows // block_len
    swap = [(0, 1), (1, 0)]

    owners = hit_owner[:, 0]
    ask = jnp.pad(jnp.concatenate([owners, hit_block]), (0, LANES - 2 * hits))
    ask = jnp.broadcast_to(ask[None, :], (peers, LANES))
    asks = lax.all_to_all(ask, "pool", split_axis=0, concat_axis=0, tiled=True)

    lat_half = lax.dynamic_slice_in_dim(pool_lat, core * half, half, axis=1)
    lat_half = lat_half.reshape(blocks, half, tiles, LANES).transpose(0, 2, 1, 3)
    rope_half = lax.dynamic_slice_in_dim(
        pool_rope, core * half * rope_width, half * rope_width, axis=1
    )
    rope_half = rope_half.reshape(blocks, 2, quarter, rope_width).transpose(0, 2, 1, 3)
    cached = jnp.concatenate(
        [
            lat_half.reshape(blocks, tiles * half, LANES),
            rope_half.reshape(blocks, quarter, 2 * rope_width),
        ],
        axis=1,
    )
    depth = cached.shape[1]

    found = pl.pallas_call(
        functools.partial(gather_kernel, hits),
        grid_spec=pltpu.PrefetchScalarGridSpec(
            num_scalar_prefetch=1,
            grid=(1,),
            in_specs=[pl.BlockSpec(memory_space=pl.ANY)],
            out_specs=pl.BlockSpec(memory_space=pl.ANY),
            scratch_shapes=[pltpu.SemaphoreType.DMA],
        ),
        out_shape=jax.ShapeDtypeStruct((peers, CAP, depth, LANES), cached.dtype),
        name="gather_hits",
    )(asks, cached)
    own = lax.all_to_all(found, "pool", split_axis=0, concat_axis=0, tiled=True)
    sib = lax.ppermute(own, "tp", swap)

    length = suffix_len[0]
    live = lax.iota(jnp.int32, rows) < length
    mine_lat = jnp.where(live[:, None], new_lat, jnp.zeros_like(new_lat))
    mine_rope = jnp.where(live[:, None], new_rope, jnp.zeros_like(new_rope))
    mine_lat = mine_lat.reshape(new_count, 2, half, latent)
    mine_lat = lax.dynamic_index_in_dim(mine_lat, core, axis=1, keepdims=False)
    rope_rows = half * rope_width // latent
    mine_rope = mine_rope.reshape(new_count, 2, rope_rows, latent)
    mine_rope = lax.dynamic_index_in_dim(mine_rope, core, axis=1, keepdims=False)
    every = jnp.concatenate([mine_lat, mine_rope], axis=1)
    source = new_place // new_count
    differs = source ^ me
    place = jnp.zeros_like(source)
    bit = peers // 2
    step = 0
    while bit:
        other = lax.ppermute(every, "pool", [(i, i ^ bit) for i in range(peers)])
        every = jnp.concatenate([every, other], axis=0)
        place = place + ((differs & bit) != 0).astype(jnp.int32) * (1 << step)
        bit //= 2
        step += 1
    chosen = every[place * new_count + new_place % new_count]
    chosen_sib = lax.ppermute(chosen, "tp", swap)
    first = jnp.where(core == 0, chosen, chosen_sib)
    second = jnp.where(core == 0, chosen_sib, chosen)
    written_lat = jnp.concatenate([first[:, :half], second[:, :half]], axis=1)
    written_rope = jnp.concatenate([first[:, half:], second[:, half:]], axis=1).reshape(
        new_place.shape[0], block_len * rope_width
    )

    q_heads = q_lat.transpose(1, 0, 2)
    qr_heads = q_rope.reshape(rows, heads, rope_width).transpose(1, 0, 2)
    group = 4
    total = hits * block_len + rows
    whole = pl.BlockSpec(memory_space=pltpu.VMEM)
    flops = 2 * heads * rows * (total * (2 * latent + rope_width) + latent * vhead)
    attn_out = pl.pallas_call(
        functools.partial(attend_kernel, block_len),
        grid_spec=pltpu.PrefetchScalarGridSpec(
            num_scalar_prefetch=2,
            grid=(heads // group,),
            in_specs=[
                whole,
                whole,
                whole,
                whole,
                pl.BlockSpec((group, rows, latent), lambda i, *_: (i, 0, 0)),
                pl.BlockSpec((group, rows, rope_width), lambda i, *_: (i, 0, 0)),
                pl.BlockSpec((group, latent, vhead), lambda i, *_: (i, 0, 0)),
            ],
            out_specs=pl.BlockSpec((rows, group * vhead), lambda i, *_: (0, i)),
            scratch_shapes=[
                pltpu.VMEM((total, latent), jnp.bfloat16),
                pltpu.VMEM((total, rope_width), jnp.bfloat16),
            ],
        ),
        out_shape=jax.ShapeDtypeStruct((rows, heads * vhead), jnp.bfloat16),
        compiler_params=pltpu.CompilerParams(vmem_limit_bytes=40 * 1024 * 1024),
        cost_estimate=pl.CostEstimate(
            flops=flops, bytes_accessed=10 * 2**20, transcendentals=heads * rows * total
        ),
        name="attend",
    )(owners, suffix_len, own, sib, new_lat, new_rope, q_heads, qr_heads, w_uv)
    return (attn_out, written_lat, written_rope)


def solution(mesh):
    return jax.shard_map(
        local,
        mesh=mesh,
        in_specs=(
            P(("groups", "pool"), "tp", None),
            P(("groups", "pool"), "tp"),
            P(("groups", "pool"), None),
            P(("groups", "pool"), None),
            P(("groups", "pool"), None, None),
            P(("groups", "pool"), None),
            P(("groups", "pool")),
            P(("groups", "pool"), None),
            P(("groups", "pool")),
            P(("groups", "pool")),
            P("tp", None, None),
        ),
        out_specs=(
            P(("groups", "pool"), "tp"),
            P(("groups", "pool"), None, None),
            P(("groups", "pool"), None),
        ),
        check_vma=False,
    )
```

time: 135 us -> 99.3 us (0.74)
  blocking collectives: 49.8 us -> 0 us
  matrix products: 21.7 us -> 0 us
  waiting for transfers between devices: 9.74 us -> 28.2 us
  Pallas kernels: 0 us -> 18.1 us
  between operations: 14.9 us -> 1.57 us
  starting transfers between devices: 14.3 us -> 27.3 us
  other arithmetic: 7.8 us -> 4.47 us
  local copies, waits for them, and re-layouts: 16.1 us -> 18.4 us
    all_gather x1 -> x0, blocking collectives: 49.8 us -> none  [local(): lax.all_gather(masked_rope, 'pool', axis=0, tiled=True)]
    ppermute x0 -> x5, waiting for transfers between devices: none -> 25.9 us  [the longest x3 25.9 us: local(): other = lax.ppermute(every, 'pool', [(i, i ^ bit) for i in range(peers)])]
    dot_general x3 -> x0, matrix products: 21.7 us -> none  [the longest x1 11.2 us: local(): jnp.einsum('shl,hlv->shv', context, w_uv, preferred_element_type=jnp.floa...]
    pallas_call x0 -> x2, Pallas kernels: none -> 18.1 us  [the longest x1 11.8 us: local(): pl.pallas_call(functools.partial(attend_kernel, block_len), grid_spec=plt...]
    all_to_all x3 -> x2, starting transfers between devices: 14.2 us -> 22.5 us  [the longest x1 15.2 us: local(): own = lax.all_to_all(found, 'pool', split_axis=0, concat_axis=0, tiled=True)]
    gather x7 -> x1, local copies, waits for them, and re-layouts: 8.77 us -> 0.55 us  [local(): chosen = every[place * new_count + new_place % new_count]]
    unnamed x12 -> x22, local copies, waits for them, and re-layouts: 6.03 us -> 13.9 us
    all_to_all x3 -> x2, waiting for transfers between devices: 9.7 us -> 2.32 us  [the longest x1 2.32 us: local(): asks = lax.all_to_all(ask, 'pool', split_axis=0, concat_axis=0, tiled=True)]
  transfers between devices with their start and end apart: 4 -> 7, of which waited for: 2 -> 4; matrix products, arithmetic and copies ran while one was open for 9% -> 16% of each run, Pallas kernels for 0% -> 0%
where the time goes in v1:
time: 99.3 us; the launch traced here: 98 us
  waiting for transfers between devices  28.2 us (28%)
  starting transfers between devices  27.3 us (27%)
  local copies, waits for them, and re-layouts  18.4 us (19%)
  Pallas kernels  18.1 us (18%)
  other arithmetic  4.47 us (5%)
  between operations  1.57 us (2%)
    ppermute x3, waiting for transfers between devices, local(): other = lax.ppermute(every, 'pool', [(i, i ^ bit) for i in range(peers)])  25.9 us
    all_to_all x1, starting transfers between devices, local(): own = lax.all_to_all(found, 'pool', split_axis=0, concat_axis=0, tiled=True)  15.2 us
    unnamed x22, local copies, waits for them, and re-layouts  13.9 us
    pallas_call x1, Pallas kernels, local(): pl.pallas_call(functools.partial(attend_kernel, block_len), grid_spec=plt...  11.8 us
    all_to_all x1, starting transfers between devices, local(): asks = lax.all_to_all(ask, 'pool', split_axis=0, concat_axis=0, tiled=True)  7.28 us
    pallas_call x1, Pallas kernels, local(): pl.pallas_call(functools.partial(gather_kernel, hits), grid_spec=pltpu.Pr...  6.34 us
    ppermute x3, starting transfers between devices, local(): other = lax.ppermute(every, 'pool', [(i, i ^ bit) for i in range(peers)])  4.59 us
    all_to_all x1, waiting for transfers between devices, local(): asks = lax.all_to_all(ask, 'pool', split_axis=0, concat_axis=0, tiled=True)  2.32 us
  transfers between devices with their start and end apart: 7, of which 4 were waited for; matrix products, arithmetic and copies ran while one was open for 16% of the time, Pallas kernels for 0%

profile of v1, /device:TPU:0, one launch (start us, length us, event | category | flops | bytes accessed | tf_op | source)
XLA Modules:
  0.0 98.0 jit_solution(18111107432061246958)
XLA Ops:
  0.6 0.0 copy-start
  0.6 0.8 pad_add_fusion
  1.5 0.6 broadcast_in_dim.33
  2.1 7.3 %all-to-all-start = ((s32[8,1,128]{2,1,0:T(1,128)}), s32[8,1,128]{2,1,0:T(1,128)S(1)}, u32[]{:S(2)}, u32[]{:S(2)}) async-start(s32[8,1,128]{2,1,0:T(1,128)} %broadcast_in_dim.33), calls=%async_computation | async-start | bytes 8192 | tf_op jit(solution)/shard_map/all_to_all | solution.py:147
  10.0 0.8 constant_dynamic-slice_fusion
  10.9 0.2 reshape.42
  11.0 0.1 copy.25
  11.2 0.1 reshape.43
  11.3 0.0 copy-done
  11.3 0.0 copy-start.6
  11.4 0.0 copy-start.2
  11.4 0.1 reshape.40
  11.5 0.1 copy.24
  11.6 0.4 copy-done.6
  12.1 0.2 copy-done.2
  12.3 0.1 broadcast_select_fusion
  12.4 0.9 pad_maximum_fusion.1.pool_ref
  13.2 0.1 copy.31
  13.3 0.1 reshape.46
  13.4 2.3 %all-to-all-done = s32[8,1,128]{2,1,0:T(1,128)S(1)} async-done(((s32[8,1,128]{2,1,0:T(1,128)}), s32[8,1,128]{2,1,0:T(1,128)S(1)}, u32[]{:S(2)}, u32[]{:S(2)}) %all-to-all-start) | async-done | bytes 4128 | tf_op jit(solution)/shard_map/all_to_all | solution.py:147
  15.8 0.0 copy-start.7
  15.8 0.6 copy-done.7
  16.3 6.3 %gather_hits.1 = bf16[8,2,144,128]{3,2,1,0:T(8,128)(2,1)} custom-call(s32[8,128]{1,0:T(8,128)} %bitcast.31, bf16[16,144,128]{2,1,0:T(8,128)(2,1)} %pad_maximum_fusion.1.pool_ref), custom_call_target="tpu_custom_call" | custom-call | tf_op jit(solution)/shard_map/gather_hits/pallas_call | solution.py:164
  22.7 0.0 copy-start.8
  22.7 15.2 %all-to-all-start.1 = ((bf16[8,2,144,128]{3,2,1,0:T(8,128)(2,1)}), bf16[8,2,144,128]{3,2,1,0:T(8,128)(2,1)S(1)}, u32[]{:S(2)}, u32[]{:S(2)}) async-start(bf16[8,2,144,128]{3,2,1,0:T(8,128)(2,1)} %gather_hits.1), calls=%async_computation.1 | async-start | bytes 1179648 | tf_op jit(solution)/shard_map/all_to_all | solution.py:176
  38.0 3.0 %collective-permute-start.1 = (bf16[2,36,512]{2,1,0:T(8,128)(2,1)S(1)}, bf16[2,36,512]{2,1,0:T(8,128)(2,1)S(1)}, u32[]{:S(2)}, u32[]{:S(2)}) collective-permute-start(bf16[2,36,512]{2,1,0:T(8,128)(2,1)S(1)} %pad_maximum_fusion.5), channel_id=1, source_target_pairs={{0,8},{2,10},{4,12},{6,14},{8,0},{10,2},{12,4},{14,6},{1,9},{3,11}... | collective-permute-start | bytes 221192 | tf_op jit(solution)/shard_map/ppermute | solution.py:195
  41.0 15.0 %collective-permute-done.1 = bf16[2,36,512]{2,1,0:T(8,128)(2,1)S(1)} collective-permute-done((bf16[2,36,512]{2,1,0:T(8,128)(2,1)S(1)}, bf16[2,36,512]{2,1,0:T(8,128)(2,1)S(1)}, u32[]{:S(2)}, u32[]{:S(2)}) %collective-permute-start.1) | collective-permute-done | bytes 73760 | tf_op jit(solution)/shard_map/ppermute | solution.py:195
  56.0 0.1 collective-permute-start.2
  56.1 5.3 %collective-permute-done.2 = bf16[4,36,512]{2,1,0:T(8,128)(2,1)S(1)} collective-permute-done((bf16[4,36,512]{2,1,0:T(8,128)(2,1)S(1)}, bf16[4,36,512]{2,1,0:T(8,128)(2,1)S(1)}, u32[]{:S(2)}, u32[]{:S(2)}) %collective-permute-start.2) | collective-permute-done | bytes 147488 | tf_op jit(solution)/shard_map/ppermute | solution.py:195
  61.4 1.5 %collective-permute-start.3 = (bf16[8,36,512]{2,1,0:T(8,128)(2,1)S(1)}, bf16[8,36,512]{2,1,0:T(8,128)(2,1)}, u32[]{:S(2)}, u32[]{:S(2)}) collective-permute-start(bf16[8,36,512]{2,1,0:T(8,128)(2,1)S(1)} %pad_maximum_fusion.2), channel_id=1, source_target_pairs={{0,2},{2,0},{4,6},{6,4},{8,10},{10,8},{12,14},{14,12},{1,3},{3,1},... | collective-permute-start | bytes 884744 | tf_op jit(solution)/shard_map/ppermute | solution.py:195
  62.9 0.0 copy-done.8
  63.0 0.0 all-to-all-done.1.own_ref
  63.0 0.1 collective-permute-start
  63.1 5.6 %collective-permute-done.3 = bf16[8,36,512]{2,1,0:T(8,128)(2,1)} collective-permute-done((bf16[8,36,512]{2,1,0:T(8,128)(2,1)S(1)}, bf16[8,36,512]{2,1,0:T(8,128)(2,1)}, u32[]{:S(2)}, u32[]{:S(2)}) %collective-permute-start.3) | collective-permute-done | bytes 294944 | tf_op jit(solution)/shard_map/ppermute | solution.py:195
  68.6 1.0 %pad_maximum_fusion = bf16[16,36,512]{2,1,0:T(8,128)(2,1)S(1)} fusion(bf16[8,36,512]{2,1,0:T(8,128)(2,1)} %collective-permute-done.3, bf16[4,36,512]{2,1,0:T(8,128)(2,1)S(1)} %collective-permute-done.2, bf16[2,36,512]{2,1,0:T(8,128)(2,1)S(1)} %collective-permute-done.1, bf16[2,4,512]{2,1,0:T(4,128)(2,1)S(1)} %dynamic-slice_bitcast_fusion.1, ...), kind=kLoop, calls=%fused_computation.2 | loop fusion | flops 2949120 | bytes 1179648 | tf_op jit(solution)/shard_map/concatenate | solution.py:196
  69.7 0.6 gather_fusion
  70.2 0.1 collective-permute-start.4
  70.3 0.1 copy.29.new_rope_ref
  70.4 0.0 copy-start.5
  70.5 6.5 %copy.35 = bf16[128,32,512]{2,0,1:T(8,128)(2,1)} copy(bf16[128,32,512]{2,1,0:T(8,128)(2,1)} %param.11) | data formatting | bytes 8388608 | tf_op args[0]
  77.0 0.0 copy-done.5
  77.0 1.0 %copy.27 = bf16[128,2048]{0,1:T(8,128)(2,1)} copy(bf16[128,2048]{1,0:T(8,128)(2,1)S(1)} %copy-done.5) | data formatting | bytes 1048576 | tf_op args[1]
  78.0 0.0 copy-start.4
  78.0 1.6 %copy.28 = bf16[128,32,64]{2,0,1:T(8,128)(2,1)S(1)} copy(bf16[128,32,64]{0,2,1:T(8,128)(2,1)} %bitcast.26) | data formatting | bytes 1048576 | tf_op jit(solution)/shard_map/reshape | solution.py:210
  79.6 0.0 collective-permute-done.4
  79.6 0.9 broadcast_select_fusion.2
  80.6 0.6 copy.33
  81.2 0.7 pad_maximum_fusion.4
  81.9 0.0 collective-permute-done.sib_ref
  81.9 0.0 copy-done.4
  81.9 0.0 copy-start.1
  81.9 2.2 %copy-done.1 = bf16[128,32,512]{2,0,1:T(8,128)(2,1)S(1)} copy-done((bf16[128,32,512]{2,0,1:T(8,128)(2,1)S(1)}, bf16[128,32,512]{2,0,1:T(8,128)(2,1)}, u32[]{:S(2)}) %copy-start.1) | copy-done | bytes 4194328
  84.0 0.0 copy-start.3
  84.0 2.2 %copy-done.3 = bf16[32,512,128]{2,1,0:T(8,128)(2,1)S(1)} copy-done((bf16[32,512,128]{2,1,0:T(8,128)(2,1)S(1)}, bf16[32,512,128]{2,1,0:T(8,128)(2,1)}, u32[]{:S(2)}) %copy-start.3) | copy-done | bytes 4194328
  86.2 11.8 %attend.1 = bf16[128,4096]{1,0:T(8,128)(2,1)} custom-call(s32[6]{0:T(128)S(1)} %bitcast.25, s32[1]{0:T(128)} %copy.36.length, bf16[8,2,144,128]{3,2,1,0:T(8,128)(2,1)S(1)} %all-to-all-done.1.own_ref, bf16[8,2,144,128]{3,2,1,0:T(8,128)(2,1)S(1)} %collective-permute-done.sib_ref, bf16[128,512]{1,0:T(8,128)(2,1)S(1)} %copy-done.2, ...), custom_call_target="tpu_custom_call" | custom-call | flops 5100273664 | bytes 10485760 | tf_op jit(solution)/shard_map/attend/pallas_call | solution.py:215
  (16 shorter events, 0.2 us)
Async XLA Ops:
  0.6 10.7 %copy-start = (bf16[16,64,512]{2,1,0:T(8,128)(2,1)S(1)}, bf16[16,64,512]{2,1,0:T(8,128)(2,1)}, u32[]{:S(2)}) copy-start(bf16[16,64,512]{2,1,0:T(8,128)(2,1)} %param.15) | copy-start | bytes 3145732
  2.1 13.7 %all-to-all-start = ((s32[8,1,128]{2,1,0:T(1,128)}), s32[8,1,128]{2,1,0:T(1,128)S(1)}, u32[]{:S(2)}, u32[]{:S(2)}) async-start(s32[8,1,128]{2,1,0:T(1,128)} %broadcast_in_dim.33), calls=%async_computation | async-start | bytes 8192 | tf_op jit(solution)/shard_map/all_to_all | solution.py:147
  11.3 0.7 copy-start.6
  11.4 0.9 copy-start.2
  15.8 0.6 copy-start.7
  22.7 40.2 %copy-start.8 = (s32[2]{0:T(128)S(1)}, s32[2]{0:T(128)}, u32[]{:S(2)}) copy-start(s32[2]{0:T(128)} %param.20) | copy-start | bytes 28
  22.7 40.3 %all-to-all-start.1 = ((bf16[8,2,144,128]{3,2,1,0:T(8,128)(2,1)}), bf16[8,2,144,128]{3,2,1,0:T(8,128)(2,1)S(1)}, u32[]{:S(2)}, u32[]{:S(2)}) async-start(bf16[8,2,144,128]{3,2,1,0:T(8,128)(2,1)} %gather_hits.1), calls=%async_computation.1 | async-start | bytes 1179648 | tf_op jit(solution)/shard_map/all_to_all | solution.py:176
  38.0 18.0 %collective-permute-start.1 = (bf16[2,36,512]{2,1,0:T(8,128)(2,1)S(1)}, bf16[2,36,512]{2,1,0:T(8,128)(2,1)S(1)}, u32[]{:S(2)}, u32[]{:S(2)}) collective-permute-start(bf16[2,36,512]{2,1,0:T(8,128)(2,1)S(1)} %pad_maximum_fusion.5), channel_id=1, source_target_pairs={{0,8},{2,10},{4,12},{6,14},{8,0},{10,2},{12,4},{14,6},{1,9},{3,11}... | collective-permute-start | bytes 221192 | tf_op jit(solution)/shard_map/ppermute | solution.py:195
  56.0 5.4 %collective-permute-start.2 = (bf16[4,36,512]{2,1,0:T(8,128)(2,1)S(1)}, bf16[4,36,512]{2,1,0:T(8,128)(2,1)S(1)}, u32[]{:S(2)}, u32[]{:S(2)}) collective-permute-start(bf16[4,36,512]{2,1,0:T(8,128)(2,1)S(1)} %pad_maximum_fusion.3), channel_id=1, source_target_pairs={{0,4},{2,6},{4,0},{6,2},{8,12},{10,14},{12,8},{14,10},{1,5},{3,7},... | collective-permute-start | bytes 442376 | tf_op jit(solution)/shard_map/ppermute | solution.py:195
  61.4 7.2 %collective-permute-start.3 = (bf16[8,36,512]{2,1,0:T(8,128)(2,1)S(1)}, bf16[8,36,512]{2,1,0:T(8,128)(2,1)}, u32[]{:S(2)}, u32[]{:S(2)}) collective-permute-start(bf16[8,36,512]{2,1,0:T(8,128)(2,1)S(1)} %pad_maximum_fusion.2), channel_id=1, source_target_pairs={{0,2},{2,0},{4,6},{6,4},{8,10},{10,8},{12,14},{14,12},{1,3},{3,1},... | collective-permute-start | bytes 884744 | tf_op jit(solution)/shard_map/ppermute | solution.py:195
  63.0 18.9 %collective-permute-start = (bf16[8,2,144,128]{3,2,1,0:T(8,128)(2,1)S(1)}, bf16[8,2,144,128]{3,2,1,0:T(8,128)(2,1)S(1)}, u32[]{:S(2)}, u32[]{:S(2)}) collective-permute-start(bf16[8,2,144,128]{3,2,1,0:T(8,128)(2,1)S(1)} %all-to-all-done.1.own_ref), channel_id=1, source_target_pairs={{0,1},{1,0},{2,3},{3,2},{4,5},{5,4},{6,7},{7,6},{8,9},{9,8},{10,11... | collective-permute-start | bytes 1769480 | tf_op jit(solution)/shard_map/ppermute | solution.py:177
  70.2 9.3 %collective-permute-start.4 = (bf16[2,36,512]{2,1,0:T(8,128)(2,1)S(1)}, bf16[2,36,512]{2,1,0:T(8,128)(2,1)}, u32[]{:S(2)}, u32[]{:S(2)}) collective-permute-start(bf16[2,36,512]{2,1,0:T(8,128)(2,1)S(1)} %gather_fusion), channel_id=1, source_target_pairs={{0,1},{1,0},{2,3},{3,2},{4,5},{5,4},{6,7},{7,6},{8,9},{9,8},{10,11... | collective-permute-start | bytes 221192 | tf_op jit(solution)/shard_map/ppermute | solution.py:201
  70.4 6.6 %copy-start.5 = (bf16[128,2048]{1,0:T(8,128)(2,1)S(1)}, bf16[128,2048]{1,0:T(8,128)(2,1)}, u32[]{:S(2)}) copy-start(bf16[128,2048]{1,0:T(8,128)(2,1)} %param.12) | copy-start | bytes 1572868
  78.0 3.9 %copy-start.4 = (s32[6,1]{0,1:T(1,128)S(1)}, s32[6,1]{0,1:T(1,128)}, u32[]{:S(2)}) copy-start(s32[6,1]{0,1:T(1,128)} %param.18) | copy-start | bytes 76
  81.9 2.2 %copy-start.1 = (bf16[128,32,512]{2,0,1:T(8,128)(2,1)S(1)}, bf16[128,32,512]{2,0,1:T(8,128)(2,1)}, u32[]{:S(2)}) copy-start(bf16[128,32,512]{2,0,1:T(8,128)(2,1)} %copy.35) | copy-start | bytes 12582916
  84.0 2.2 %copy-start.3 = (bf16[32,512,128]{2,1,0:T(8,128)(2,1)S(1)}, bf16[32,512,128]{2,1,0:T(8,128)(2,1)}, u32[]{:S(2)}) copy-start(bf16[32,512,128]{2,1,0:T(8,128)(2,1)} %w_ref.1) | copy-start | bytes 12582916

commit v2 on v1

--- a/solution.py
+++ b/solution.py
@@ -14,31 +14,22 @@
 exp2_scale = softmax_scale / math.log(2.0)
 
 
-def gather_kernel(hits, asks, pool_ref, out_ref, sem):
+def gather_kernel(hits, asks, pool_ref, out_ref):
     me = lax.axis_index("pool")
-    peers = out_ref.shape[0]
-
-    def each_request(fn):
-        def body(r, carry):
-            rank = jnp.int32(0)
-            for k in range(hits):
-                mine = asks[r, k] == me
-
-                @pl.when(mine)
-                def _(rank=rank, k=k):
-                    fn(r, rank, asks[r, hits + k])
-
-                rank = rank + mine.astype(jnp.int32)
-            return carry
-
-        lax.fori_loop(0, peers, body, 0)
-
-    def copy(r, rank, block):
-        slot = jnp.minimum(rank, CAP - 1)
-        return pltpu.make_async_copy(pool_ref.at[block], out_ref.at[r, slot], sem)
-
-    each_request(lambda r, rank, block: copy(r, rank, block).start())
-    each_request(lambda r, rank, block: copy(r, rank, block).wait())
+
+    def body(r, carry):
+        rank = jnp.int32(0)
+        wanted = [jnp.int32(0)] * CAP
+        for k in range(hits):
+            mine = (asks[r, k] == me).astype(jnp.int32)
+            for s in range(CAP):
+                wanted[s] = jnp.where((rank == s) & (mine == 1), asks[r, hits + k], wanted[s])
+            rank = rank + mine
+        for s in range(CAP):
+            out_ref[r, s] = pool_ref[wanted[s]]
+        return carry
+
+    lax.fori_loop(0, out_ref.shape[0], body, 0)
 
 
 def attend_kernel(
@@ -161,21 +152,6 @@
     )
     depth = cached.shape[1]
 
-    found = pl.pallas_call(
-        functools.partial(gather_kernel, hits),
-        grid_spec=pltpu.PrefetchScalarGridSpec(
-            num_scalar_prefetch=1,
-            grid=(1,),
-            in_specs=[pl.BlockSpec(memory_space=pl.ANY)],
-            out_specs=pl.BlockSpec(memory_space=pl.ANY),
-            scratch_shapes=[pltpu.SemaphoreType.DMA],
-        ),
-        out_shape=jax.ShapeDtypeStruct((peers, CAP, depth, LANES), cached.dtype),
-        name="gather_hits",
-    )(asks, cached)
-    own = lax.all_to_all(found, "pool", split_axis=0, concat_axis=0, tiled=True)
-    sib = lax.ppermute(own, "tp", swap)
-
     length = suffix_len[0]
     live = lax.iota(jnp.int32, rows) < length
     mine_lat = jnp.where(live[:, None], new_lat, jnp.zeros_like(new_lat))
@@ -186,11 +162,34 @@
     mine_rope = mine_rope.reshape(new_count, 2, rope_rows, latent)
     mine_rope = lax.dynamic_index_in_dim(mine_rope, core, axis=1, keepdims=False)
     every = jnp.concatenate([mine_lat, mine_rope], axis=1)
+    bit = peers // 2
+    other = lax.ppermute(every, "pool", [(i, i ^ bit) for i in range(peers)])
+    asks, every, other = lax.optimization_barrier((asks, every, other))
+    every = jnp.concatenate([every, other], axis=0)
+
+    found = pl.pallas_call(
+        functools.partial(gather_kernel, hits),
+        grid_spec=pltpu.PrefetchScalarGridSpec(
+            num_scalar_prefetch=1,
+            grid=(1,),
+            in_specs=[pl.BlockSpec(memory_space=pltpu.VMEM)],
+            out_specs=pl.BlockSpec(memory_space=pltpu.VMEM),
+        ),
+        out_shape=jax.ShapeDtypeStruct((peers, CAP, depth, LANES), cached.dtype),
+        compiler_params=pltpu.CompilerParams(vmem_limit_bytes=16 * 1024 * 1024),
+        name="gather_hits",
+    )(asks, cached)
+    own = lax.all_to_all(found, "pool", split_axis=0, concat_axis=0, tiled=True)
+    q_heads = q_lat.transpose(1, 0, 2)
+    qr_heads = q_rope.reshape(rows, heads, rope_width).transpose(1, 0, 2)
+    own, q_heads, qr_heads = lax.optimization_barrier((own, q_heads, qr_heads))
+    sib = lax.ppermute(own, "tp", swap)
+
     source = new_place // new_count
     differs = source ^ me
-    place = jnp.zeros_like(source)
-    bit = peers // 2
-    step = 0
+    place = ((differs & bit) != 0).astype(jnp.int32)
+    bit //= 2
+    step = 1
     while bit:
         other = lax.ppermute(every, "pool", [(i, i ^ bit) for i in range(peers)])
         every = jnp.concatenate([every, other], axis=0)
@@ -206,8 +205,6 @@
         new_place.shape[0], block_len * rope_width
     )
 
-    q_heads = q_lat.transpose(1, 0, 2)
-    qr_heads = q_rope.reshape(rows, heads, rope_width).transpose(1, 0, 2)
     group = 4
     total = hits * block_len + rows
     whole = pl.BlockSpec(memory_space=pltpu.VMEM)
@@ -233,7 +230,7 @@
             ],
         ),
         out_shape=jax.ShapeDtypeStruct((rows, heads * vhead), jnp.bfloat16),
-        compiler_params=pltpu.CompilerParams(vmem_limit_bytes=40 * 1024 * 1024),
+        compiler_params=pltpu.CompilerParams(vmem_limit_bytes=60 * 1024 * 1024),
         cost_estimate=pl.CostEstimate(
             flops=flops, bytes_accessed=10 * 2**20, transcendentals=heads * rows * total
         ),

time: 99.3 us -> 63.9 us (0.64)
  waiting for transfers between devices: 28.2 us -> 9.99 us
  starting transfers between devices: 27.3 us -> 20.5 us
  local copies, waits for them, and re-layouts: 18.4 us -> 12.4 us
  Pallas kernels: 18.1 us -> 15.4 us
    ppermute x3, waiting for transfers between devices: 25.9 us -> 9.45 us  [local(): other = lax.ppermute(every, 'pool', [(i, i ^ bit) for i in range(peers)])]
    all_to_all x1, starting transfers between devices: 15.2 us -> 6.28 us  [local(): own = lax.all_to_all(found, 'pool', split_axis=0, concat_axis=0, tiled=True)]
    unnamed x22 -> x14, local copies, waits for them, and re-layouts: 13.9 us -> 8.14 us
    pallas_call x1, Pallas kernels: 6.34 us -> 1.64 us  [local(): pl.pallas_call(functools.partial(gather_kernel, hits), grid_spec=pltpu.Pr...]
    all_to_all x1, waiting for transfers between devices: 2.32 us -> 0.01 us  [local(): asks = lax.all_to_all(ask, 'pool', split_axis=0, concat_axis=0, tiled=True)]
    ppermute x3, starting transfers between devices: 4.59 us -> 6.84 us  [local(): other = lax.ppermute(every, 'pool', [(i, i ^ bit) for i in range(peers)])]
    pallas_call x1, Pallas kernels: 11.8 us -> 13.7 us  [local(): pl.pallas_call(functools.partial(attend_kernel, block_len), grid_spec=plt...]
  transfers between devices with their start and end apart: 7 -> 7, of which waited for: 4 -> 4; matrix products, arithmetic and copies ran while one was open for 16% -> 23% of each run, Pallas kernels for 0% -> 0%
where the time goes in v2:
time: 63.9 us; the launch traced here: 63.4 us
  starting transfers between devices  20.5 us (32%)
  Pallas kernels  15.4 us (24%)
  local copies, waits for them, and re-layouts  12.4 us (19%)
  waiting for transfers between devices  9.99 us (16%)
  other arithmetic  3.52 us (6%)
  between operations  1.53 us (2%)
    pallas_call x1, Pallas kernels, local(): pl.pallas_call(functools.partial(attend_kernel, block_len), grid_spec=plt...  13.7 us
    ppermute x3, waiting for transfers between devices, local(): other = lax.ppermute(every, 'pool', [(i, i ^ bit) for i in range(peers)])  9.45 us
    unnamed x14, local copies, waits for them, and re-layouts  8.14 us
    all_to_all x1, starting transfers between devices, local(): asks = lax.all_to_all(ask, 'pool', split_axis=0, concat_axis=0, tiled=True)  7.28 us
    ppermute x3, starting transfers between devices, local(): other = lax.ppermute(every, 'pool', [(i, i ^ bit) for i in range(peers)])  6.84 us
    all_to_all x1, starting transfers between devices, local(): own = lax.all_to_all(found, 'pool', split_axis=0, concat_axis=0, tiled=True)  6.28 us
    pallas_call x1, Pallas kernels, local(): pl.pallas_call(functools.partial(gather_kernel, hits), grid_spec=pltpu.Pr...  1.64 us
    reshape x1, local copies, waits for them, and re-layouts, local(): qr_heads = q_rope.reshape(rows, heads, rope_width).transpose(1, 0, 2)  1.34 us
  transfers between devices with their start and end apart: 7, of which 4 were waited for; matrix products, arithmetic and copies ran while one was open for 23% of the time, Pallas kernels for 0%

profile of v2, /device:TPU:0, one launch (start us, length us, event | category | flops | bytes accessed | tf_op | source)
XLA Modules:
  0.0 63.4 jit_solution(13475647470804843869)
XLA Ops:
  0.6 0.0 copy-start
  0.6 0.8 %pad_add_fusion = s32[12]{0:T(128)S(1)} fusion(s32[6]{0:T(128)} %param.17, s32[6]{0:T(128)} %bitcast.31), kind=kLoop, calls=%fused_computation.30 | loop fusion | flops 12 | bytes 96 | tf_op jit(solution)/shard_map/concatenate | solution.py:136
  1.5 0.6 broadcast_in_dim.33
  2.1 7.3 %all-to-all-start = ((s32[8,1,128]{2,1,0:T(1,128)}), s32[8,1,128]{2,1,0:T(1,128)S(1)}, u32[]{:S(2)}, u32[]{:S(2)}) async-start(s32[8,1,128]{2,1,0:T(1,128)} %broadcast_in_dim.33), calls=%async_computation | async-start | bytes 8192 | tf_op jit(solution)/shard_map/all_to_all | solution.py:138
  10.0 0.7 %broadcast_select_fusion.3 = bf16[128,64]{0,1:T(8,128)(2,1)S(1)} fusion(bf16[128,64]{0,1:T(8,128)(2,1)} %param.14, pred[128]{0:T(512)(128)(4,1)S(1)} %iota_compare_fusion), kind=kLoop, calls=%fused_computation.13 | loop fusion | flops 8192 | bytes 32896 | tf_op jit(solution)/shard_map/jit(_where)/select_n | solution.py:158
  10.8 0.1 copy.25
  10.9 0.1 reshape.41
  11.0 0.0 copy-start.2
  11.0 1.0 %broadcast_select_fusion = bf16[128,512]{1,0:T(8,128)(2,1)S(1)} fusion(bf16[128,512]{1,0:T(8,128)(2,1)} %new_lat_ref.1, pred[128]{0:T(512)(128)(4,1)S(1)} %iota_compare_fusion), kind=kLoop, calls=%fused_computation.7 | loop fusion | flops 65536 | bytes 262272 | tf_op jit(solution)/shard_map/jit(_where)/select_n | solution.py:157
  12.1 3.0 %collective-permute-start = (bf16[2,36,512]{2,1,0:T(8,128)(2,1)S(1)}, bf16[2,36,512]{2,1,0:T(8,128)(2,1)S(1)}, u32[]{:S(2)}, u32[]{:S(2)}) collective-permute-start(bf16[2,36,512]{2,1,0:T(8,128)(2,1)S(1)} %pad_maximum_fusion.5), channel_id=1, source_target_pairs={{0,8},{2,10},{4,12},{6,14},{8,0},{10,2},{12,4},{14,6},{1,9},{3,11}... | collective-permute-start | bytes 221192 | tf_op jit(solution)/shard_map/ppermute | solution.py:166
  15.1 0.8 %constant_dynamic-slice_fusion = bf16[16,2048]{1,0:T(8,128)(2,1)S(1)} fusion(bf16[16,4096]{1,0:T(8,128)(2,1)} %param.16, s32[]{:T(128)S(6)} %select_n.51), kind=kLoop, calls=%fused_computation.25 | loop fusion | bytes 131076 | tf_op jit(solution)/shard_map/dynamic_slice | solution.py:142
  15.9 0.2 reshape.44
  16.1 0.1 copy.27
  16.2 0.1 reshape.45
  16.4 0.0 copy-done
  16.4 0.1 reshape.42
  16.5 0.1 copy.26
  16.7 0.0 all-to-all-done
  16.7 1.5 %collective-permute-done = bf16[2,36,512]{2,1,0:T(8,128)(2,1)S(1)} collective-permute-done((bf16[2,36,512]{2,1,0:T(8,128)(2,1)S(1)}, bf16[2,36,512]{2,1,0:T(8,128)(2,1)S(1)}, u32[]{:S(2)}, u32[]{:S(2)}) %collective-permute-start) | collective-permute-done | bytes 73760 | tf_op jit(solution)/shard_map/ppermute | solution.py:166
  18.2 1.6 %gather_hits.1 = bf16[8,2,144,128]{3,2,1,0:T(8,128)(2,1)} custom-call(s32[8,128]{1,0:T(8,128)S(1)} %bitcast.22, bf16[16,144,128]{2,1,0:T(8,128)(2,1)S(1)} %pad_maximum_fusion.1.pool_ref), custom_call_target="tpu_custom_call" | custom-call | tf_op jit(solution)/shard_map/gather_hits/pallas_call | solution.py:170
  19.8 6.3 %all-to-all-start.1 = ((bf16[8,2,144,128]{3,2,1,0:T(8,128)(2,1)}), bf16[8,2,144,128]{3,2,1,0:T(8,128)(2,1)S(1)}, u32[]{:S(2)}, u32[]{:S(2)}) async-start(bf16[8,2,144,128]{3,2,1,0:T(8,128)(2,1)} %gather_hits.1), calls=%async_computation.1 | async-start | bytes 1179648 | tf_op jit(solution)/shard_map/all_to_all | solution.py:182
  26.1 2.1 %collective-permute-start.2 = (bf16[4,36,512]{2,1,0:T(8,128)(2,1)S(1)}, bf16[4,36,512]{2,1,0:T(8,128)(2,1)S(1)}, u32[]{:S(2)}, u32[]{:S(2)}) collective-permute-start(bf16[4,36,512]{2,1,0:T(8,128)(2,1)S(1)} %pad_maximum_fusion.3), channel_id=1, source_target_pairs={{0,4},{2,6},{4,0},{6,2},{8,12},{10,14},{12,8},{14,10},{1,5},{3,7},... | collective-permute-start | bytes 442376 | tf_op jit(solution)/shard_map/ppermute | solution.py:194
  28.2 0.0 copy-done.2
  28.2 0.3 copy.29
  28.5 1.3 %copy.30 = bf16[128,32,64]{2,0,1:T(8,128)(2,1)} copy(bf16[128,32,64]{0,2,1:T(8,128)(2,1)S(1)} %bitcast.24) | data formatting | bytes 1048576 | tf_op jit(solution)/shard_map/reshape | solution.py:184
  29.8 0.0 copy-start.4
  29.8 0.0 copy-start.3
  29.8 6.5 %copy.35 = bf16[128,32,512]{2,0,1:T(8,128)(2,1)} copy(bf16[128,32,512]{2,1,0:T(8,128)(2,1)} %param.11) | data formatting | bytes 8388608 | tf_op args[0]
  36.3 2.8 %collective-permute-done.2 = bf16[4,36,512]{2,1,0:T(8,128)(2,1)S(1)} collective-permute-done((bf16[4,36,512]{2,1,0:T(8,128)(2,1)S(1)}, bf16[4,36,512]{2,1,0:T(8,128)(2,1)S(1)}, u32[]{:S(2)}, u32[]{:S(2)}) %collective-permute-start.2) | collective-permute-done | bytes 147488 | tf_op jit(solution)/shard_map/ppermute | solution.py:194
  39.1 1.8 %collective-permute-start.3 = (bf16[8,36,512]{2,1,0:T(8,128)(2,1)S(1)}, bf16[8,36,512]{2,1,0:T(8,128)(2,1)S(1)}, u32[]{:S(2)}, u32[]{:S(2)}) collective-permute-start(bf16[8,36,512]{2,1,0:T(8,128)(2,1)S(1)} %pad_maximum_fusion.2), channel_id=1, source_target_pairs={{0,2},{2,0},{4,6},{6,4},{8,10},{10,8},{12,14},{14,12},{1,3},{3,1},... | collective-permute-start | bytes 884744 | tf_op jit(solution)/shard_map/ppermute | solution.py:194
  40.9 0.0 copy-done.4
  40.9 0.0 all-to-all-done.1.own_ref
  40.9 0.0 copy-start.1
  40.9 0.1 collective-permute-start.1
  41.0 5.2 %collective-permute-done.3 = bf16[8,36,512]{2,1,0:T(8,128)(2,1)S(1)} collective-permute-done((bf16[8,36,512]{2,1,0:T(8,128)(2,1)S(1)}, bf16[8,36,512]{2,1,0:T(8,128)(2,1)S(1)}, u32[]{:S(2)}, u32[]{:S(2)}) %collective-permute-start.3) | collective-permute-done | bytes 294944 | tf_op jit(solution)/shard_map/ppermute | solution.py:194
  46.3 0.1 pad_maximum_fusion
  46.3 0.6 gather_fusion
  46.9 0.1 collective-permute-start.4
  47.0 0.0 copy-done.3
  47.0 0.7 %copy.31.new_rope_ref = bf16[128,64]{1,0:T(8,128)(2,1)} copy(bf16[128,64]{0,1:T(8,128)(2,1)S(1)} %copy-done.3) | data formatting | bytes 32768 | tf_op args[3]
  47.7 0.5 collective-permute-done.4
  48.3 0.6 copy.33
  49.0 0.7 %pad_maximum_fusion.4 = bf16[2,64,512]{2,1,0:T(8,128)(2,1)} fusion(bf16[2,32,512]{2,1,0:T(8,128)(2,1)S(1)} %slice.19, bf16[2,32,512]{2,1,0:T(8,128)(2,1)S(1)} %slice.18), kind=kLoop, calls=%fused_computation.6 | loop fusion | flops 262144 | bytes 262144 | tf_op jit(solution)/shard_map/concatenate | solution.py:203
  49.6 0.0 collective-permute-done.1.sib_ref
  49.6 0.0 copy-done.1
  49.6 13.7 %attend.1 = bf16[128,4096]{1,0:T(8,128)(2,1)} custom-call(s32[6]{0:T(128)} %bitcast.32, s32[1]{0:T(128)} %copy.36.length, bf16[8,2,144,128]{3,2,1,0:T(8,128)(2,1)} %copy-done.1, bf16[8,2,144,128]{3,2,1,0:T(8,128)(2,1)} %collective-permute-done.1.sib_ref, bf16[128,512]{1,0:T(8,128)(2,1)} %new_lat_ref.1, bf16[128,64]{1,0:T(8,128)(2,1)} %copy.31.new_rope_ref, ...), custom_call_target="tpu_custom_call" | custom-call | flops 5100273664 | bytes 10485760 | tf_op jit(solution)/shard_map/attend/pallas_call | solution.py:212
  (17 shorter events, 0.3 us)
Async XLA Ops:
  0.6 15.7 %copy-start = (bf16[16,64,512]{2,1,0:T(8,128)(2,1)S(1)}, bf16[16,64,512]{2,1,0:T(8,128)(2,1)}, u32[]{:S(2)}) copy-start(bf16[16,64,512]{2,1,0:T(8,128)(2,1)} %param.15) | copy-start | bytes 3145732
  2.1 14.6 %all-to-all-start = ((s32[8,1,128]{2,1,0:T(1,128)}), s32[8,1,128]{2,1,0:T(1,128)S(1)}, u32[]{:S(2)}, u32[]{:S(2)}) async-start(s32[8,1,128]{2,1,0:T(1,128)} %broadcast_in_dim.33), calls=%async_computation | async-start | bytes 8192 | tf_op jit(solution)/shard_map/all_to_all | solution.py:138
  11.0 17.2 %copy-start.2 = (bf16[128,2048]{1,0:T(8,128)(2,1)S(1)}, bf16[128,2048]{1,0:T(8,128)(2,1)}, u32[]{:S(2)}) copy-start(bf16[128,2048]{1,0:T(8,128)(2,1)} %param.12) | copy-start | bytes 1572868
  12.1 6.1 %collective-permute-start = (bf16[2,36,512]{2,1,0:T(8,128)(2,1)S(1)}, bf16[2,36,512]{2,1,0:T(8,128)(2,1)S(1)}, u32[]{:S(2)}, u32[]{:S(2)}) collective-permute-start(bf16[2,36,512]{2,1,0:T(8,128)(2,1)S(1)} %pad_maximum_fusion.5), channel_id=1, source_target_pairs={{0,8},{2,10},{4,12},{6,14},{8,0},{10,2},{12,4},{14,6},{1,9},{3,11}... | collective-permute-start | bytes 221192 | tf_op jit(solution)/shard_map/ppermute | solution.py:166
  19.8 21.1 %all-to-all-start.1 = ((bf16[8,2,144,128]{3,2,1,0:T(8,128)(2,1)}), bf16[8,2,144,128]{3,2,1,0:T(8,128)(2,1)S(1)}, u32[]{:S(2)}, u32[]{:S(2)}) async-start(bf16[8,2,144,128]{3,2,1,0:T(8,128)(2,1)} %gather_hits.1), calls=%async_computation.1 | async-start | bytes 1179648 | tf_op jit(solution)/shard_map/all_to_all | solution.py:182
  26.1 13.0 %collective-permute-start.2 = (bf16[4,36,512]{2,1,0:T(8,128)(2,1)S(1)}, bf16[4,36,512]{2,1,0:T(8,128)(2,1)S(1)}, u32[]{:S(2)}, u32[]{:S(2)}) collective-permute-start(bf16[4,36,512]{2,1,0:T(8,128)(2,1)S(1)} %pad_maximum_fusion.3), channel_id=1, source_target_pairs={{0,4},{2,6},{4,0},{6,2},{8,12},{10,14},{12,8},{14,10},{1,5},{3,7},... | collective-permute-start | bytes 442376 | tf_op jit(solution)/shard_map/ppermute | solution.py:194
  29.8 11.1 %copy-start.4 = (s32[2]{0:T(128)S(1)}, s32[2]{0:T(128)}, u32[]{:S(2)}) copy-start(s32[2]{0:T(128)} %param.20) | copy-start | bytes 28
  29.8 17.2 %copy-start.3 = (bf16[128,64]{0,1:T(8,128)(2,1)S(1)}, bf16[128,64]{0,1:T(8,128)(2,1)}, u32[]{:S(2)}) copy-start(bf16[128,64]{0,1:T(8,128)(2,1)} %param.14) | copy-start | bytes 49156
  39.1 7.1 %collective-permute-start.3 = (bf16[8,36,512]{2,1,0:T(8,128)(2,1)S(1)}, bf16[8,36,512]{2,1,0:T(8,128)(2,1)S(1)}, u32[]{:S(2)}, u32[]{:S(2)}) collective-permute-start(bf16[8,36,512]{2,1,0:T(8,128)(2,1)S(1)} %pad_maximum_fusion.2), channel_id=1, source_target_pairs={{0,2},{2,0},{4,6},{6,4},{8,10},{10,8},{12,14},{14,12},{1,3},{3,1},... | collective-permute-start | bytes 884744 | tf_op jit(solution)/shard_map/ppermute | solution.py:194
  40.9 8.7 %copy-start.1 = (bf16[8,2,144,128]{3,2,1,0:T(8,128)(2,1)}, bf16[8,2,144,128]{3,2,1,0:T(8,128)(2,1)S(1)}, u32[]{:S(2)}) copy-start(bf16[8,2,144,128]{3,2,1,0:T(8,128)(2,1)S(1)} %all-to-all-done.1.own_ref) | copy-start | bytes 1769476
  40.9 8.7 %collective-permute-start.1 = (bf16[8,2,144,128]{3,2,1,0:T(8,128)(2,1)S(1)}, bf16[8,2,144,128]{3,2,1,0:T(8,128)(2,1)}, u32[]{:S(2)}, u32[]{:S(2)}) collective-permute-start(bf16[8,2,144,128]{3,2,1,0:T(8,128)(2,1)S(1)} %all-to-all-done.1.own_ref), channel_id=1, source_target_pairs={{0,1},{1,0},{2,3},{3,2},{4,5},{5,4},{6,7},{7,6},{8,9},{9,8},{10,11... | collective-permute-start | bytes 1769480 | tf_op jit(solution)/shard_map/ppermute | solution.py:186
  46.9 1.3 %collective-permute-start.4 = (bf16[2,36,512]{2,1,0:T(8,128)(2,1)S(1)}, bf16[2,36,512]{2,1,0:T(8,128)(2,1)S(1)}, u32[]{:S(2)}, u32[]{:S(2)}) collective-permute-start(bf16[2,36,512]{2,1,0:T(8,128)(2,1)S(1)} %gather_fusion), channel_id=1, source_target_pairs={{0,1},{1,0},{2,3},{3,2},{4,5},{5,4},{6,7},{7,6},{8,9},{9,8},{10,11... | collective-permute-start | bytes 221192 | tf_op jit(solution)/shard_map/ppermute | solution.py:200

commit v3 on v2

v3 whole, which is shorter than its diff:
```python
import functools
import math

import jax
import jax.numpy as jnp
from jax import lax
from jax.experimental import pallas as pl
from jax.experimental.pallas import tpu as pltpu
from jax.sharding import PartitionSpec as P

CAP = 2
LANES = 128
softmax_scale = 1.0 / math.sqrt(192.0)
exp2_scale = softmax_scale / math.log(2.0)


def gather_kernel(hits, asks, pool_ref, out_ref):
    me = lax.axis_index("pool")

    def body(r, carry):
        rank = jnp.int32(0)
        wanted = [jnp.int32(0)] * CAP
        for k in range(hits):
            mine = (asks[r, k] == me).astype(jnp.int32)
            for s in range(CAP):
                wanted[s] = jnp.where((rank == s) & (mine == 1), asks[r, hits + k], wanted[s])
            rank = rank + mine
        for s in range(CAP):
            out_ref[r, s] = pool_ref[wanted[s]]
        return carry

    lax.fori_loop(0, out_ref.shape[0], body, 0)


def ask_kernel(block_len, *refs):
    sources, out_ref, held = refs[:6], refs[6], refs[7:13]
    tokens, rows32, sems = refs[13:]
    copies = [
        pltpu.make_async_copy(source, dest, sems.at[i])
        for i, (source, dest) in enumerate(zip(sources, held))
    ]
    for copy in copies:
        copy.start()
    for copy in copies:
        copy.wait()
    hit_block, hit_owner, length, new_place, lat_ref, rope_ref = held
    core = lax.axis_index("tp")
    pieces = out_ref.shape[0]
    latent = lat_ref.shape[1]
    tiles = latent // LANES
    half = block_len // 2
    part = half // (pieces // tiles)
    new_count = lat_ref.shape[0] // block_len
    hits = hit_block.shape[0]
    pairs = half // 2 // pieces

    lane = lax.broadcasted_iota(jnp.int32, (1, LANES), 1)
    ask = jnp.zeros((1, LANES), jnp.int32)
    for k in range(hits):
        ask = jnp.where(lane == k, hit_owner[k], ask)
        ask = jnp.where(lane == hits + k, hit_block[k], ask)
    for s in range(new_count):
        ask = jnp.where(lane == 2 * hits + s, new_place[s], ask)
    ask = ask.astype(jnp.float32)

    token_keep = lax.broadcasted_iota(jnp.int32, tokens.shape, 0) < length[0]
    tokens[...] = jnp.where(token_keep, rope_ref[...].astype(jnp.float32).T, 0.0)
    for b in range(new_count):
        base = b * block_len + core * half
        at = pl.multiple_of(base, half)
        keep = lax.broadcasted_iota(jnp.int32, (half, latent), 0) + base < length[0]
        lat = jnp.where(keep, lat_ref[pl.ds(at, half), :].astype(jnp.float32), 0.0)
        lat = lat.astype(out_ref.dtype)
        for j in range(pieces):
            u, t = j // tiles, j % tiles
            out_ref[j, b * part : (b + 1) * part, :] = lat[
                u * part : (u + 1) * part, t * LANES : (t + 1) * LANES
            ]
        even = tokens[pl.ds(at, half // 2, stride=2), :]
        odd = tokens[pl.ds(at + 1, half // 2, stride=2), :]
        paired = jnp.concatenate([even, odd], axis=1)
        for j in range(pieces):
            for p in range(pairs):
                row = p * new_count + b
                g = j * pairs + p
                rows32[j, row : row + 1, :] = paired[g : g + 1]
    filled = pairs * new_count
    for j in range(pieces):
        rows32[j, filled:8, :] = jnp.zeros((8 - filled, LANES), jnp.float32)
        rows32[j, 8:16, :] = jnp.broadcast_to(ask, (8, LANES))
        out_ref[j, new_count * part :, :] = rows32[j].astype(out_ref.dtype)


def answer_kernel(hits, new_count, asks_ref, pool_ref, out_ref, rows32, ids_vec, ids, sem):
    me = lax.axis_index("pool")
    peers, depth = out_ref.shape[0], pool_ref.shape[1]
    tail = asks_ref.shape[1] - 16
    part = tail // new_count
    for r in range(peers):
        tile = asks_ref[r, tail:, :].astype(jnp.float32)
        rows32[r] = tile
        ids_vec[r : r + 1, :] = tile[8:9].astype(jnp.int32)
    copy = pltpu.make_async_copy(ids_vec, ids, sem)
    copy.start()
    copy.wait()
    pairs_row = lax.broadcasted_iota(jnp.int32, (8, LANES), 0)

    def body(r, carry):
        rank = jnp.int32(0)
        wanted = [jnp.int32(0)] * CAP
        for k in range(hits):
            mine = (ids[r, k] == me).astype(jnp.int32)
            for s in range(CAP):
                wanted[s] = jnp.where((rank == s) & (mine == 1), ids[r, hits + k], wanted[s])
            rank = rank + mine
        for s in range(CAP):
            out_ref[r, s * depth : (s + 1) * depth, :] = pool_ref[wanted[s]]
        base = CAP * depth
        merged = jnp.zeros((8, LANES), jnp.float32)
        for s in range(new_count):
            place = ids[r, 2 * hits + s]
            source, block = place // new_count, place % new_count
            out_ref[r, base + s * part : base + (s + 1) * part, :] = asks_ref[
                source, pl.ds(pl.multiple_of(block * part, part), part), :
            ]
            tile = rows32[source, 0:8, :]
            shifted = tile
            for move in range(1, new_count):
                up = pltpu.roll(tile, 8 - move, 0)
                down = pltpu.roll(tile, move, 0)
                shifted = jnp.where(block - s == move, up, shifted)
                shifted = jnp.where(s - block == move, down, shifted)
            merged = jnp.where(pairs_row % new_count == s, shifted, merged)
        both = jnp.concatenate([merged, jnp.zeros((8, LANES), jnp.float32)], axis=0)
        out_ref[r, base + tail :, :] = both.astype(out_ref.dtype)
        return carry

    lax.fori_loop(0, peers, body, 0)


def write_back(block_len, base, own_ref, sib_ref, lat_ref, rope_ref):
    core = lax.axis_index("tp")
    pieces = own_ref.shape[0]
    slots, _, latent = lat_ref.shape
    tiles = latent // LANES
    half = block_len // 2
    part = half // (pieces // tiles)
    pairs = half // 2 // pieces
    sides = []
    for side, ref in enumerate((own_ref, sib_ref)):
        start = pl.multiple_of((core if side == 0 else 1 - core) * half, half)
        row = []
        for j in range(pieces):
            u, t = j // tiles, j % tiles
            for s in range(slots):
                lat_ref[s, pl.ds(start + u * part, part), t * LANES : (t + 1) * LANES] = ref[
                    j, base + s * part : base + (s + 1) * part, :
                ]
            tile = ref[j, base + slots * part :, :].astype(jnp.float32)
            for p in range(pairs):
                row.append(tile[p * slots : (p + 1) * slots])
        sides.append(jnp.concatenate(row, axis=1))
    first = jnp.where(core == 0, sides[0], sides[1])
    second = jnp.where(core == 0, sides[1], sides[0])
    rope_ref[...] = jnp.concatenate([first, second], axis=1).astype(rope_ref.dtype)


def suffix_kernel(group, lat_ref, rope_ref, *refs):
    sources, (out_ref, done_ref), held, sems = refs[:2], refs[2:4], refs[4:6], refs[6]
    q_ref, qr_ref = held
    heads, rows, latent = q_ref.shape
    steps = heads // group

    def arrive(g, a):
        at = pl.ds(g * group, group)
        return pltpu.make_async_copy(sources[a].at[at], held[a].at[at], sems.at[g, a])

    for g in range(steps):
        arrive(g, 0).start()
        arrive(g, 1).start()
    position = lax.broadcasted_iota(jnp.int32, (group, rows, rows), 1)
    key_at = lax.broadcasted_iota(jnp.int32, (group, rows, rows), 2)
    for g in range(steps):
        arrive(g, 0).wait()
        arrive(g, 1).wait()
        at = slice(g * group, (g + 1) * group)
        q = q_ref[at].reshape(group * rows, latent)
        qr = qr_ref[at].reshape(group * rows, qr_ref.shape[2])
        scores = lax.dot_general(
            q, lat_ref[...], (((1,), (1,)), ((), ())), preferred_element_type=jnp.float32
        )
        scores = scores + jnp.dot(qr, rope_ref[...], preferred_element_type=jnp.float32)
        out_ref[at] = jnp.where(key_at <= position, scores.reshape(group, rows, rows), -1e30)
    done_ref[...] = jnp.zeros_like(done_ref)


def attend_kernel(
    block_len, owners, length, own_ref, sib_ref, done_ref, new_lat_ref, q_ref, qr_ref, tail_ref, w_ref, *refs
):
    out_ref, *written = refs[:-2]
    keys, rope = refs[-2:]
    hits = owners.shape[0]
    group, rows, latent = q_ref.shape
    rope_width = qr_ref.shape[2]
    width = w_ref.shape[2]
    half = block_len // 2
    quarter = half // 2
    prefix = hits * block_len
    tiles = latent // LANES
    depth = tiles * half + quarter

    @pl.when(pl.program_id(0) == 0)
    def _():
        for k in range(hits):
            owner = owners[k]
            rank = jnp.int32(0)
            for j in range(k):
                rank = rank + (owners[j] == owner).astype(jnp.int32)
            slot = pl.multiple_of(jnp.minimum(rank, CAP - 1) * depth, 16)
            for side, ref in enumerate((own_ref, sib_ref)):
                block = ref.at[owner, pl.ds(slot, depth), :]
                base = k * block_len + side * half
                for t in range(tiles):
                    keys[base : base + half, t * LANES : (t + 1) * LANES] = block[
                        t * half : (t + 1) * half, :
                    ]
                packed = block[tiles * half : tiles * half + quarter, :]
                rope[base : base + quarter, :] = packed[:, :rope_width]
                rope[base + quarter : base + half, :] = packed[:, rope_width:]
        keys[prefix:, :] = new_lat_ref[...]
        if written:
            write_back(block_len, depth * CAP, own_ref, sib_ref, *written)

    contract = (((1,), (1,)), ((), ()))
    live = lax.broadcasted_iota(jnp.int32, (rows, width), 0) < length[0]
    q = q_ref[...].reshape(group * rows, latent)
    qr = qr_ref[...].reshape(group * rows, rope_width)
    scores = lax.dot_general(q, keys[:prefix, :], contract, preferred_element_type=jnp.float32)
    scores = scores + lax.dot_general(
        qr, rope[...], contract, preferred_element_type=jnp.float32
    )
    scores = jnp.concatenate([scores, tail_ref[...].reshape(group * rows, rows)], axis=1)
    top = jnp.max(scores, axis=1, keepdims=True)
    parts = jnp.exp2((scores - top) * exp2_scale)
    norm = 1.0 / jnp.sum(parts, axis=1, keepdims=True)
    weights = (parts * norm).astype(jnp.bfloat16)
    context = jnp.dot(weights, keys[...], preferred_element_type=jnp.float32)
    context = context.astype(jnp.bfloat16)
    for h in range(group):
        value = jnp.dot(
            context[h * rows : (h + 1) * rows], w_ref[h], preferred_element_type=jnp.float32
        )
        out_ref[:, h * width : (h + 1) * width] = jnp.where(live, value, 0.0).astype(
            out_ref.dtype
        )


def local(
    q_lat,
    q_rope,
    new_lat,
    new_rope,
    pool_lat,
    pool_rope,
    hit_block,
    hit_owner,
    suffix_len,
    new_place,
    w_uv,
):
    peers = lax.axis_size("pool")
    me = lax.axis_index("pool")
    core = lax.axis_index("tp")
    cores = lax.axis_size("tp")
    assert cores == 2
    hits = hit_block.shape[0]
    blocks, block_len, latent = pool_lat.shape
    rows, rope_width = new_rope.shape
    half = block_len // 2
    quarter = half // 2
    tiles = latent // LANES
    heads = q_lat.shape[1]
    vhead = w_uv.shape[2]
    new_count = rows // block_len
    swap = [(0, 1), (1, 0)]

    owners = hit_owner[:, 0]
    whole = pl.BlockSpec(memory_space=pltpu.VMEM)
    anywhere = pl.BlockSpec(memory_space=pl.ANY)
    part = half * tiles // peers
    two_hops = peers % tiles == 0 and part % 16 == 0 and half % (2 * peers) == 0

    lat_half = lax.dynamic_slice_in_dim(pool_lat, core * half, half, axis=1)
    lat_half = lat_half.reshape(blocks, half, tiles, LANES).transpose(0, 2, 1, 3)
    rope_half = lax.dynamic_slice_in_dim(
        pool_rope, core * half * rope_width, half * rope_width, axis=1
    )
    rope_half = rope_half.reshape(blocks, 2, quarter, rope_width).transpose(0, 2, 1, 3)
    cached = jnp.concatenate(
        [
            lat_half.reshape(blocks, tiles * half, LANES),
            rope_half.reshape(blocks, quarter, 2 * rope_width),
        ],
        axis=1,
    )
    depth = cached.shape[1]

    if two_hops:
        asked = pl.pallas_call(
            functools.partial(ask_kernel, block_len),
            in_specs=[anywhere] * 6,
            out_specs=whole,
            scratch_shapes=[
                pltpu.SMEM((hits,), jnp.int32),
                pltpu.SMEM((hits,), jnp.int32),
                pltpu.SMEM((1,), jnp.int32),
                pltpu.SMEM(new_place.shape, jnp.int32),
                pltpu.VMEM((rows, latent), new_lat.dtype),
                pltpu.VMEM((rope_width, rows), new_rope.dtype),
                pltpu.VMEM((rows, rope_width), jnp.float32),
                pltpu.VMEM((peers, 16, LANES), jnp.float32),
                pltpu.SemaphoreType.DMA((6,)),
            ],
            out_shape=jax.ShapeDtypeStruct((peers, new_count * part + 16, LANES), new_lat.dtype),
            compiler_params=pltpu.CompilerParams(vmem_limit_bytes=60 * 1024 * 1024),
            name="ask",
        )(hit_block, owners, suffix_len, new_place, new_lat, new_rope.T)
        asks = lax.all_to_all(asked, "pool", split_axis=0, concat_axis=0, tiled=True)
        found = pl.pallas_call(
            functools.partial(answer_kernel, hits, new_count),
            in_specs=[whole] * 2,
            out_specs=whole,
            scratch_shapes=[
                pltpu.VMEM((peers, 16, LANES), jnp.float32),
                pltpu.VMEM((peers, LANES), jnp.int32),
                pltpu.SMEM((peers, LANES), jnp.int32),
                pltpu.SemaphoreType.DMA,
            ],
            out_shape=jax.ShapeDtypeStruct(
                (peers, CAP * depth + new_count * part + 16, LANES), cached.dtype
            ),
            compiler_params=pltpu.CompilerParams(vmem_limit_bytes=8 * 1024 * 1024),
            name="answer",
        )(asks, cached)
        own = lax.all_to_all(found, "pool", split_axis=0, concat_axis=0, tiled=True)
    else:
        ask = jnp.pad(jnp.concatenate([owners, hit_block]), (0, LANES - 2 * hits))
        ask = jnp.broadcast_to(ask[None, :], (peers, LANES))
        asks = lax.all_to_all(ask, "pool", split_axis=0, concat_axis=0, tiled=True)

        length = suffix_len[0]
        live = lax.iota(jnp.int32, rows) < length
        mine_lat = jnp.where(live[:, None], new_lat, jnp.zeros_like(new_lat))
        mine_rope = jnp.where(live[:, None], new_rope, jnp.zeros_like(new_rope))
        mine_lat = mine_lat.reshape(new_count, 2, half, latent)
        mine_lat = lax.dynamic_index_in_dim(mine_lat, core, axis=1, keepdims=False)
        rope_rows = half * rope_width // latent
        mine_rope = mine_rope.reshape(new_count, 2, rope_rows, latent)
        mine_rope = lax.dynamic_index_in_dim(mine_rope, core, axis=1, keepdims=False)
        every = jnp.concatenate([mine_lat, mine_rope], axis=1)
        bit = peers // 2
        other = lax.ppermute(every, "pool", [(i, i ^ bit) for i in range(peers)])
        asks, every, other = lax.optimization_barrier((asks, every, other))
        every = jnp.concatenate([every, other], axis=0)

        found = pl.pallas_call(
            functools.partial(gather_kernel, hits),
            grid_spec=pltpu.PrefetchScalarGridSpec(
                num_scalar_prefetch=1,
                grid=(1,),
                in_specs=[pl.BlockSpec(memory_space=pltpu.VMEM)],
                out_specs=pl.BlockSpec(memory_space=pltpu.VMEM),
            ),
            out_shape=jax.ShapeDtypeStruct((peers, CAP, depth, LANES), cached.dtype),
            compiler_params=pltpu.CompilerParams(vmem_limit_bytes=16 * 1024 * 1024),
            name="gather_hits",
        )(asks, cached)
        found = found.reshape(peers, CAP * depth, LANES)
        own = lax.all_to_all(found, "pool", split_axis=0, concat_axis=0, tiled=True)
    q_heads = q_lat.transpose(1, 0, 2)
    qr_heads = q_rope.reshape(rows, heads, rope_width).transpose(1, 0, 2)
    group = 8
    tail, done = pl.pallas_call(
        functools.partial(suffix_kernel, group),
        in_specs=[whole] * 2 + [anywhere] * 2,
        out_specs=[whole] * 2,
        out_shape=[
            jax.ShapeDtypeStruct((heads, rows, rows), jnp.float32),
            jax.ShapeDtypeStruct((8, LANES), jnp.float32),
        ],
        scratch_shapes=[
            pltpu.VMEM(q_heads.shape, q_heads.dtype),
            pltpu.VMEM(qr_heads.shape, qr_heads.dtype),
            pltpu.SemaphoreType.DMA((heads // group, 2)),
        ],
        compiler_params=pltpu.CompilerParams(vmem_limit_bytes=58 * 1024 * 1024),
        cost_estimate=pl.CostEstimate(
            flops=2 * heads * rows * rows * (latent + rope_width),
            bytes_accessed=12 * 2**20,
            transcendentals=0,
        ),
        name="suffix",
    )(new_lat, new_rope.T, q_heads, qr_heads)
    own, done = lax.optimization_barrier((own, done))
    sib = lax.ppermute(own, "tp", swap)
    if not two_hops:
        source = new_place // new_count
        differs = source ^ me
        place = ((differs & bit) != 0).astype(jnp.int32)
        bit //= 2
        step = 1
        while bit:
            other = lax.ppermute(every, "pool", [(i, i ^ bit) for i in range(peers)])
            every = jnp.concatenate([every, other], axis=0)
            place = place + ((differs & bit) != 0).astype(jnp.int32) * (1 << step)
            bit //= 2
            step += 1
        chosen = every[place * new_count + new_place % new_count]
        chosen_sib = lax.ppermute(chosen, "tp", swap)
        first = jnp.where(core == 0, chosen, chosen_sib)
        second = jnp.where(core == 0, chosen_sib, chosen)
        written_lat = jnp.concatenate([first[:, :half], second[:, :half]], axis=1)
        written_rope = jnp.concatenate([first[:, half:], second[:, half:]], axis=1).reshape(
            new_place.shape[0], block_len * rope_width
        )

    total = hits * block_len + rows
    flops = 2 * heads * rows * (total * (2 * latent + rope_width) + latent * vhead)
    out_specs = [pl.BlockSpec((rows, group * vhead), lambda i, *_: (0, i))]
    out_shape = [jax.ShapeDtypeStruct((rows, heads * vhead), jnp.bfloat16)]
    if two_hops:
        slots = new_place.shape[0]
        for shape in ((slots, block_len, latent), (slots, block_len * rope_width)):
            out_specs.append(whole)
            out_shape.append(jax.ShapeDtypeStruct(shape, new_lat.dtype))
    streamed = [
        pl.BlockSpec((group,) + x.shape[1:], lambda i, *_: (i, 0, 0))
        for x in (q_heads, qr_heads, tail, w_uv)
    ]
    attn_out, *written = pl.pallas_call(
        functools.partial(attend_kernel, block_len),
        grid_spec=pltpu.PrefetchScalarGridSpec(
            num_scalar_prefetch=2,
            grid=(heads // group,),
            in_specs=[whole] * 4 + streamed,
            out_specs=out_specs,
            scratch_shapes=[
                pltpu.VMEM((total, latent), jnp.bfloat16),
                pltpu.VMEM((hits * block_len, rope_width), jnp.bfloat16),
            ],
        ),
        out_shape=out_shape,
        compiler_params=pltpu.CompilerParams(vmem_limit_bytes=60 * 1024 * 1024),
        cost_estimate=pl.CostEstimate(
            flops=flops, bytes_accessed=10 * 2**20, transcendentals=heads * rows * total
        ),
        name="attend",
    )(owners, suffix_len, own, sib, done, new_lat, q_heads, qr_heads, tail, w_uv)
    if two_hops:
        written_lat, written_rope = written
    return (attn_out, written_lat, written_rope)


def solution(mesh):
    return jax.shard_map(
        local,
        mesh=mesh,
        in_specs=(
            P(("groups", "pool"), "tp", None),
            P(("groups", "pool"), "tp"),
            P(("groups", "pool"), None),
            P(("groups", "pool"), None),
            P(("groups", "pool"), None, None),
            P(("groups", "pool"), None),
            P(("groups", "pool")),
            P(("groups", "pool"), None),
            P(("groups", "pool")),
            P(("groups", "pool")),
            P("tp", None, None),
        ),
        out_specs=(
            P(("groups", "pool"), "tp"),
            P(("groups", "pool"), None, None),
            P(("groups", "pool"), None),
        ),
        check_vma=False,
    )
```

time: 63.9 us -> 56 us (0.88)
  starting transfers between devices: 20.5 us -> 10.9 us
  Pallas kernels: 15.4 us -> 22 us
  other arithmetic: 3.52 us -> 0.04 us
  local copies, waits for them, and re-layouts: 12.4 us -> 10.5 us
  waiting for transfers between devices: 9.99 us -> 10.7 us
    ppermute x4 -> x0, waiting for transfers between devices: 9.98 us -> none  [the longest x3 9.45 us: local(): other = lax.ppermute(every, 'pool', [(i, i ^ bit) for i in range(peers)])]
    pallas_call x1 -> x3, Pallas kernels: 1.64 us -> 9.33 us  [the longest x1 5.71 us: local(): pl.pallas_call(functools.partial(suffix_kernel, group), in_specs=[whole]...]
    ppermute x4 -> x0, starting transfers between devices: 6.91 us -> none  [the longest x3 6.84 us: local(): other = lax.ppermute(every, 'pool', [(i, i ^ bit) for i in range(peers)])]
    all_to_all x1, waiting for transfers between devices: 0.01 us -> 5.52 us  [local(): lax.all_to_all(asked, 'pool', split_axis=0, concat_axis=0, tiled=True)]
    all_to_all x1, waiting for transfers between devices: 0.01 us -> 3.08 us  [local(): own = lax.all_to_all(found, 'pool', split_axis=0, concat_axis=0, tiled=True)]
    all_to_all x1, starting transfers between devices: 6.28 us -> 3.56 us  [local(): own = lax.all_to_all(found, 'pool', split_axis=0, concat_axis=0, tiled=True)]
    ppermute x1, waiting for transfers between devices: 0.01 us -> 2.14 us  [local(): sib = lax.ppermute(own, 'tp', swap)]
    select_n x4 -> x0, other arithmetic: 1.81 us -> none  [the longest x1 1.05 us: local(): mine_lat = jnp.where(live[:, None], new_lat, jnp.zeros_like(new_lat))]
  transfers between devices with their start and end apart: 7 -> 3, of which waited for: 4 -> 3; matrix products, arithmetic and copies ran while one was open for 23% -> 17% of each run, Pallas kernels for 0% -> 10%
where the time goes in v3:
time: 56 us; the launch traced here: 55.6 us
  Pallas kernels  22 us (39%)
  starting transfers between devices  10.9 us (19%)
  waiting for transfers between devices  10.7 us (19%)
  local copies, waits for them, and re-layouts  10.5 us (19%)
  between operations  1.49 us (3%)
    pallas_call x1, Pallas kernels, local(): pl.pallas_call(functools.partial(attend_kernel, block_len), grid_spec=plt...  12.7 us
    unnamed x10, local copies, waits for them, and re-layouts  7.69 us
    all_to_all x1, starting transfers between devices, local(): lax.all_to_all(asked, 'pool', split_axis=0, concat_axis=0, tiled=True)  7.29 us
    pallas_call x1, Pallas kernels, local(): pl.pallas_call(functools.partial(suffix_kernel, group), in_specs=[whole]...  5.71 us
    all_to_all x1, waiting for transfers between devices, local(): lax.all_to_all(asked, 'pool', split_axis=0, concat_axis=0, tiled=True)  5.52 us
    all_to_all x1, starting transfers between devices, local(): own = lax.all_to_all(found, 'pool', split_axis=0, concat_axis=0, tiled=True)  3.56 us
    all_to_all x1, waiting for transfers between devices, local(): own = lax.all_to_all(found, 'pool', split_axis=0, concat_axis=0, tiled=True)  3.08 us
    ppermute x1, waiting for transfers between devices, local(): sib = lax.ppermute(own, 'tp', swap)  2.14 us
  transfers between devices with their start and end apart: 3, of which 3 were waited for; matrix products, arithmetic and copies ran while one was open for 17% of the time, Pallas kernels for 10%

profile of v3, /device:TPU:0, one launch (start us, length us, event | category | flops | bytes accessed | tf_op | source)
XLA Modules:
  0.0 55.6 jit_solution(4825843509938759447)
XLA Ops:
  0.6 0.0 copy-start
  1.4 1.8 %ask.1 = bf16[8,48,128]{2,1,0:T(8,128)(2,1)} custom-call(s32[6]{0:T(128)} %refs_0_.1, s32[6]{0:T(128)} %bitcast.20, s32[1]{0:T(128)S(6)} %copy.22.refs_2_.length, s32[2]{0:T(128)} %refs_3_.1, bf16[128,512]{1,0:T(8,128)(2,1)} %new_lat_ref.1, bf16[64,128]{1,0:T(8,128)(2,1)} %bitcast.18), custom_call_target="tpu_custom_call" | custom-call | tf_op jit(solution)/shard_map/ask/pallas_call | solution.py:309
  3.2 7.3 %all-to-all-start = ((bf16[8,48,128]{2,1,0:T(8,128)(2,1)}), bf16[8,48,128]{2,1,0:T(8,128)(2,1)S(1)}, u32[]{:S(2)}, u32[]{:S(2)}) async-start(bf16[8,48,128]{2,1,0:T(8,128)(2,1)} %ask.1), calls=%async_computation | async-start | bytes 196608 | tf_op jit(solution)/shard_map/all_to_all | solution.py:328
  10.5 0.8 %constant_dynamic-slice_fusion = bf16[16,2048]{1,0:T(8,128)(2,1)S(1)} fusion(bf16[16,4096]{1,0:T(8,128)(2,1)} %param.16, s32[]{:T(128)S(6)} %select_n.7), kind=kLoop, calls=%fused_computation.2 | loop fusion | bytes 131076 | tf_op jit(solution)/shard_map/dynamic_slice | solution.py:295
  11.3 0.0 copy-done
  11.4 0.2 reshape.23
  11.5 0.1 copy.16
  11.7 0.1 reshape.24
  11.8 0.1 reshape.21
  11.9 0.1 copy.15
  12.0 0.0 copy-start.2
  12.1 5.5 %all-to-all-done.asks_ref = bf16[8,48,128]{2,1,0:T(8,128)(2,1)S(1)} async-done(((bf16[8,48,128]{2,1,0:T(8,128)(2,1)}), bf16[8,48,128]{2,1,0:T(8,128)(2,1)S(1)}, u32[]{:S(2)}, u32[]{:S(2)}) %all-to-all-start) | async-done | bytes 98336 | tf_op jit(solution)/shard_map/all_to_all | solution.py:328
  17.6 1.8 %answer.1 = bf16[8,336,128]{2,1,0:T(8,128)(2,1)} custom-call(bf16[8,48,128]{2,1,0:T(8,128)(2,1)S(1)} %all-to-all-done.asks_ref, bf16[16,144,128]{2,1,0:T(8,128)(2,1)S(1)} %pad_maximum_fusion.pool_ref), custom_call_target="tpu_custom_call" | custom-call | tf_op jit(solution)/shard_map/answer/pallas_call | solution.py:329
  19.4 3.6 %all-to-all-start.1 = ((bf16[8,336,128]{2,1,0:T(8,128)(2,1)}), bf16[8,336,128]{2,1,0:T(8,128)(2,1)S(1)}, u32[]{:S(2)}, u32[]{:S(2)}) async-start(bf16[8,336,128]{2,1,0:T(8,128)(2,1)} %answer.1), calls=%async_computation.1 | async-start | bytes 1376256 | tf_op jit(solution)/shard_map/all_to_all | solution.py:345
  23.0 0.0 copy-done.2
  23.0 0.3 copy.18
  23.3 1.4 %copy.19 = bf16[128,32,64]{2,0,1:T(8,128)(2,1)} copy(bf16[128,32,64]{0,2,1:T(8,128)(2,1)S(1)} %bitcast.14) | data formatting | bytes 1048576 | tf_op jit(solution)/shard_map/reshape | solution.py:381
  24.6 6.5 %copy.21 = bf16[128,32,512]{2,0,1:T(8,128)(2,1)} copy(bf16[128,32,512]{2,1,0:T(8,128)(2,1)} %param.11) | data formatting | bytes 8388608 | tf_op args[0]
  31.1 5.7 %suffix.1 = (f32[32,128,128]{2,1,0:T(8,128)}, f32[8,128]{1,0:T(8,128)}) custom-call(bf16[128,512]{1,0:T(8,128)(2,1)} %new_lat_ref.1, bf16[64,128]{1,0:T(8,128)(2,1)} %bitcast.19, bf16[32,128,512]{2,1,0:T(8,128)(2,1)} %bitcast.10, bf16[32,128,64]{2,1,0:T(8,128)(2,1)} %bitcast.12), custom_call_target="tpu_custom_call" | custom-call | flops 603979776 | bytes 12582912 | tf_op jit(solution)/shard_map/suffix/pallas_call | solution.py:383
  36.8 3.1 %all-to-all-done.1.own_ref = bf16[8,336,128]{2,1,0:T(8,128)(2,1)S(1)} async-done(((bf16[8,336,128]{2,1,0:T(8,128)(2,1)}), bf16[8,336,128]{2,1,0:T(8,128)(2,1)S(1)}, u32[]{:S(2)}, u32[]{:S(2)}) %all-to-all-start.1) | async-done | bytes 688160 | tf_op jit(solution)/shard_map/all_to_all | solution.py:345
  39.9 0.0 copy-start.1
  39.9 0.0 collective-permute-start
  39.9 2.1 %collective-permute-done.sib_ref = bf16[8,336,128]{2,1,0:T(8,128)(2,1)S(1)} collective-permute-done((bf16[8,336,128]{2,1,0:T(8,128)(2,1)S(1)}, bf16[8,336,128]{2,1,0:T(8,128)(2,1)S(1)}, u32[]{:S(2)}, u32[]{:S(2)}) %collective-permute-start) | collective-permute-done | bytes 688160 | tf_op jit(solution)/shard_map/ppermute | solution.py:405
  42.1 0.0 copy-start.3
  42.1 0.0 copy-done.1
  42.1 0.9 %copy-done.3 = bf16[8,336,128]{2,1,0:T(8,128)(2,1)} copy-done((bf16[8,336,128]{2,1,0:T(8,128)(2,1)}, bf16[8,336,128]{2,1,0:T(8,128)(2,1)S(1)}, u32[]{:S(2)}) %copy-start.3) | copy-done | bytes 688152
  43.0 12.7 %attend.1 = (bf16[128,4096]{1,0:T(8,128)(2,1)}, bf16[2,64,512]{2,1,0:T(8,128)(2,1)}, bf16[2,4096]{1,0:T(2,128)(2,1)}) custom-call(s32[6]{0:T(128)} %bitcast.21, s32[1]{0:T(128)S(6)} %copy.22.refs_2_.length, bf16[8,336,128]{2,1,0:T(8,128)(2,1)} %copy-done.1, bf16[8,336,128]{2,1,0:T(8,128)(2,1)} %copy-done.3, f32[8,128]{1,0:T(8,128)} %get-tuple-element.9.done_ref, ...), custom_call_target="tpu_custom_call" | custom-call | flops 5100273664 | bytes 10485760 | tf_op jit(solution)/shard_map/attend/pallas_call | solution.py:440
  (2 shorter events, 0.1 us)
Async XLA Ops:
  0.6 10.7 %copy-start = (bf16[16,64,512]{2,1,0:T(8,128)(2,1)S(1)}, bf16[16,64,512]{2,1,0:T(8,128)(2,1)}, u32[]{:S(2)}) copy-start(bf16[16,64,512]{2,1,0:T(8,128)(2,1)} %param.15) | copy-start | bytes 3145732
  3.2 14.4 %all-to-all-start = ((bf16[8,48,128]{2,1,0:T(8,128)(2,1)}), bf16[8,48,128]{2,1,0:T(8,128)(2,1)S(1)}, u32[]{:S(2)}, u32[]{:S(2)}) async-start(bf16[8,48,128]{2,1,0:T(8,128)(2,1)} %ask.1), calls=%async_computation | async-start | bytes 196608 | tf_op jit(solution)/shard_map/all_to_all | solution.py:328
  12.0 11.0 %copy-start.2 = (bf16[128,2048]{1,0:T(8,128)(2,1)S(1)}, bf16[128,2048]{1,0:T(8,128)(2,1)}, u32[]{:S(2)}) copy-start(bf16[128,2048]{1,0:T(8,128)(2,1)} %param.12) | copy-start | bytes 1572868
  19.4 20.5 %all-to-all-start.1 = ((bf16[8,336,128]{2,1,0:T(8,128)(2,1)}), bf16[8,336,128]{2,1,0:T(8,128)(2,1)S(1)}, u32[]{:S(2)}, u32[]{:S(2)}) async-start(bf16[8,336,128]{2,1,0:T(8,128)(2,1)} %answer.1), calls=%async_computation.1 | async-start | bytes 1376256 | tf_op jit(solution)/shard_map/all_to_all | solution.py:345
  39.9 2.2 %copy-start.1 = (bf16[8,336,128]{2,1,0:T(8,128)(2,1)}, bf16[8,336,128]{2,1,0:T(8,128)(2,1)S(1)}, u32[]{:S(2)}) copy-start(bf16[8,336,128]{2,1,0:T(8,128)(2,1)S(1)} %all-to-all-done.1.own_ref) | copy-start | bytes 2064388
  39.9 2.1 %collective-permute-start = (bf16[8,336,128]{2,1,0:T(8,128)(2,1)S(1)}, bf16[8,336,128]{2,1,0:T(8,128)(2,1)S(1)}, u32[]{:S(2)}, u32[]{:S(2)}) collective-permute-start(bf16[8,336,128]{2,1,0:T(8,128)(2,1)S(1)} %all-to-all-done.1.own_ref), channel_id=1, source_target_pairs={{0,1},{1,0},{2,3},{3,2},{4,5},{5,4},{6,7},{7,6},{8,9},{9,8},{10,11... | collective-permute-start | bytes 2064392 | tf_op jit(solution)/shard_map/ppermute | solution.py:405
  42.1 0.9 %copy-start.3 = (bf16[8,336,128]{2,1,0:T(8,128)(2,1)}, bf16[8,336,128]{2,1,0:T(8,128)(2,1)S(1)}, u32[]{:S(2)}) copy-start(bf16[8,336,128]{2,1,0:T(8,128)(2,1)S(1)} %collective-permute-done.sib_ref) | copy-start | bytes 2064388

commit v4 on v3

--- a/solution.py
+++ b/solution.py
@@ -166,7 +166,7 @@
 
 
 def suffix_kernel(group, lat_ref, rope_ref, *refs):
-    sources, (out_ref, done_ref), held, sems = refs[:2], refs[2:4], refs[4:6], refs[6]
+    sources, out_ref, held, sems = refs[:2], refs[2], refs[3:5], refs[5]
     q_ref, qr_ref = held
     heads, rows, latent = q_ref.shape
     steps = heads // group
@@ -191,15 +191,13 @@
         )
         scores = scores + jnp.dot(qr, rope_ref[...], preferred_element_type=jnp.float32)
         out_ref[at] = jnp.where(key_at <= position, scores.reshape(group, rows, rows), -1e30)
-    done_ref[...] = jnp.zeros_like(done_ref)
 
 
 def attend_kernel(
-    block_len, owners, length, own_ref, sib_ref, done_ref, new_lat_ref, q_ref, qr_ref, tail_ref, w_ref, *refs
+    block_len, hits, numbers, own_ref, sib_ref, new_lat_ref, q_ref, qr_ref, tail_ref, w_ref, *refs
 ):
     out_ref, *written = refs[:-2]
     keys, rope = refs[-2:]
-    hits = owners.shape[0]
     group, rows, latent = q_ref.shape
     rope_width = qr_ref.shape[2]
     width = w_ref.shape[2]
@@ -212,10 +210,10 @@
     @pl.when(pl.program_id(0) == 0)
     def _():
         for k in range(hits):
-            owner = owners[k]
+            owner = numbers[k]
             rank = jnp.int32(0)
             for j in range(k):
-                rank = rank + (owners[j] == owner).astype(jnp.int32)
+                rank = rank + (numbers[j] == owner).astype(jnp.int32)
             slot = pl.multiple_of(jnp.minimum(rank, CAP - 1) * depth, 16)
             for side, ref in enumerate((own_ref, sib_ref)):
                 block = ref.at[owner, pl.ds(slot, depth), :]
@@ -232,27 +230,40 @@
             write_back(block_len, depth * CAP, own_ref, sib_ref, *written)
 
     contract = (((1,), (1,)), ((), ()))
-    live = lax.broadcasted_iota(jnp.int32, (rows, width), 0) < length[0]
-    q = q_ref[...].reshape(group * rows, latent)
-    qr = qr_ref[...].reshape(group * rows, rope_width)
-    scores = lax.dot_general(q, keys[:prefix, :], contract, preferred_element_type=jnp.float32)
-    scores = scores + lax.dot_general(
-        qr, rope[...], contract, preferred_element_type=jnp.float32
-    )
-    scores = jnp.concatenate([scores, tail_ref[...].reshape(group * rows, rows)], axis=1)
-    top = jnp.max(scores, axis=1, keepdims=True)
-    parts = jnp.exp2((scores - top) * exp2_scale)
-    norm = 1.0 / jnp.sum(parts, axis=1, keepdims=True)
-    weights = (parts * norm).astype(jnp.bfloat16)
-    context = jnp.dot(weights, keys[...], preferred_element_type=jnp.float32)
-    context = context.astype(jnp.bfloat16)
-    for h in range(group):
-        value = jnp.dot(
-            context[h * rows : (h + 1) * rows], w_ref[h], preferred_element_type=jnp.float32
+    live = lax.broadcasted_iota(jnp.int32, (rows, width), 0) < numbers[hits]
+    some = 4
+
+    def score(i):
+        at = slice(i * some, (i + 1) * some)
+        q = q_ref[at].reshape(some * rows, latent)
+        qr = qr_ref[at].reshape(some * rows, rope_width)
+        scores = lax.dot_general(q, keys[:prefix, :], contract, preferred_element_type=jnp.float32)
+        scores = scores + lax.dot_general(
+            qr, rope[...], contract, preferred_element_type=jnp.float32
         )
-        out_ref[:, h * width : (h + 1) * width] = jnp.where(live, value, 0.0).astype(
-            out_ref.dtype
-        )
+        return jnp.concatenate([scores, tail_ref[at].reshape(some * rows, rows)], axis=1)
+
+    def finish(i, scores):
+        top = jnp.max(scores, axis=1, keepdims=True)
+        parts = jnp.exp2((scores - top) * exp2_scale)
+        norm = 1.0 / jnp.sum(parts, axis=1, keepdims=True)
+        weights = (parts * norm).astype(jnp.bfloat16)
+        context = jnp.dot(weights, keys[...], preferred_element_type=jnp.float32)
+        context = context.astype(jnp.bfloat16)
+        for h in range(some):
+            value = jnp.dot(
+                context[h * rows : (h + 1) * rows],
+                w_ref[i * some + h],
+                preferred_element_type=jnp.float32,
+            )
+            lanes = slice((i * some + h) * width, (i * some + h + 1) * width)
+            out_ref[:, lanes] = jnp.where(live, value, 0.0).astype(out_ref.dtype)
+
+    scores = score(0)
+    for i in range(group // some):
+        later = score(i + 1) if (i + 1) * some < group else None
+        finish(i, scores)
+        scores = later
 
 
 def local(
@@ -380,14 +391,11 @@
     q_heads = q_lat.transpose(1, 0, 2)
     qr_heads = q_rope.reshape(rows, heads, rope_width).transpose(1, 0, 2)
     group = 8
-    tail, done = pl.pallas_call(
+    tail = pl.pallas_call(
         functools.partial(suffix_kernel, group),
         in_specs=[whole] * 2 + [anywhere] * 2,
-        out_specs=[whole] * 2,
-        out_shape=[
-            jax.ShapeDtypeStruct((heads, rows, rows), jnp.float32),
-            jax.ShapeDtypeStruct((8, LANES), jnp.float32),
-        ],
+        out_specs=whole,
+        out_shape=jax.ShapeDtypeStruct((heads, rows, rows), jnp.float32),
         scratch_shapes=[
             pltpu.VMEM(q_heads.shape, q_heads.dtype),
             pltpu.VMEM(qr_heads.shape, qr_heads.dtype),
@@ -401,7 +409,7 @@
         ),
         name="suffix",
     )(new_lat, new_rope.T, q_heads, qr_heads)
-    own, done = lax.optimization_barrier((own, done))
+    own, tail = lax.optimization_barrier((own, tail))
     sib = lax.ppermute(own, "tp", swap)
     if not two_hops:
         source = new_place // new_count
@@ -438,11 +446,11 @@
         for x in (q_heads, qr_heads, tail, w_uv)
     ]
     attn_out, *written = pl.pallas_call(
-        functools.partial(attend_kernel, block_len),
+        functools.partial(attend_kernel, block_len, hits),
         grid_spec=pltpu.PrefetchScalarGridSpec(
-            num_scalar_prefetch=2,
+            num_scalar_prefetch=1,
             grid=(heads // group,),
-            in_specs=[whole] * 4 + streamed,
+            in_specs=[whole] * 3 + streamed,
             out_specs=out_specs,
             scratch_shapes=[
                 pltpu.VMEM((total, latent), jnp.bfloat16),
@@ -450,12 +458,12 @@
             ],
         ),
         out_shape=out_shape,
-        compiler_params=pltpu.CompilerParams(vmem_limit_bytes=60 * 1024 * 1024),
+        compiler_params=pltpu.CompilerParams(vmem_limit_bytes=52 * 1024 * 1024),
         cost_estimate=pl.CostEstimate(
             flops=flops, bytes_accessed=10 * 2**20, transcendentals=heads * rows * total
         ),
         name="attend",
-    )(owners, suffix_len, own, sib, done, new_lat, q_heads, qr_heads, tail, w_uv)
+    )(jnp.concatenate([owners, suffix_len]), own, sib, new_lat, q_heads, qr_heads, tail, w_uv)
     if two_hops:
         written_lat, written_rope = written
     return (attn_out, written_lat, written_rope)

time: 56 us -> 53 us (0.946)
  Pallas kernels: 22 us -> 19.8 us
  local copies, waits for them, and re-layouts: 10.5 us -> 9.61 us
    pallas_call x1, Pallas kernels: 12.7 us -> 10.4 us  [local(): pl.pallas_call(functools.partial(attend_kernel, block_len, hits), grid_sp...]
    unnamed x10, local copies, waits for them, and re-layouts: 7.69 us -> 6.76 us
  transfers between devices with their start and end apart: 3 -> 3, of which waited for: 3 -> 3; matrix products, arithmetic and copies ran while one was open for 17% -> 18% of each run, Pallas kernels for 10% -> 11%
where the time goes in v4:
time: 53 us; the launch traced here: 52.5 us
  Pallas kernels  19.8 us (37%)
  starting transfers between devices  10.9 us (21%)
  waiting for transfers between devices  10.6 us (20%)
  local copies, waits for them, and re-layouts  9.61 us (18%)
  between operations  1.49 us (3%)
    pallas_call x1, Pallas kernels, local(): pl.pallas_call(functools.partial(attend_kernel, block_len, hits), grid_sp...  10.4 us
    all_to_all x1, starting transfers between devices, local(): lax.all_to_all(asked, 'pool', split_axis=0, concat_axis=0, tiled=True)  7.29 us
    unnamed x10, local copies, waits for them, and re-layouts  6.76 us
    pallas_call x1, Pallas kernels, local(): pl.pallas_call(functools.partial(suffix_kernel, group), in_specs=[whole]...  5.78 us
    all_to_all x1, waiting for transfers between devices, local(): lax.all_to_all(asked, 'pool', split_axis=0, concat_axis=0, tiled=True)  5.52 us
    all_to_all x1, starting transfers between devices, local(): own = lax.all_to_all(found, 'pool', split_axis=0, concat_axis=0, tiled=True)  3.56 us
    all_to_all x1, waiting for transfers between devices, local(): own = lax.all_to_all(found, 'pool', split_axis=0, concat_axis=0, tiled=True)  3.01 us
    ppermute x1, waiting for transfers between devices, local(): sib = lax.ppermute(own, 'tp', swap)  2.06 us
  transfers between devices with their start and end apart: 3, of which 3 were waited for; matrix products, arithmetic and copies ran while one was open for 18% of the time, Pallas kernels for 11%

profile of v4, /device:TPU:0, one launch (start us, length us, event | category | flops | bytes accessed | tf_op | source)
XLA Modules:
  0.0 52.5 jit_solution(1232602134198828376)
XLA Ops:
  0.6 0.0 copy-start
  1.4 1.8 %ask.1 = bf16[8,48,128]{2,1,0:T(8,128)(2,1)} custom-call(s32[6]{0:T(128)} %refs_0_.1, s32[6]{0:T(128)} %bitcast.20, s32[1]{0:T(128)S(6)} %copy.22.refs_2_, s32[2]{0:T(128)} %refs_3_.1, bf16[128,512]{1,0:T(8,128)(2,1)} %new_lat_ref.1, bf16[64,128]{1,0:T(8,128)(2,1)} %bitcast.18), custom_call_target="tpu_custom_call" | custom-call | tf_op jit(solution)/shard_map/ask/pallas_call | solution.py:320
  3.2 7.3 %all-to-all-start = ((bf16[8,48,128]{2,1,0:T(8,128)(2,1)}), bf16[8,48,128]{2,1,0:T(8,128)(2,1)S(1)}, u32[]{:S(2)}, u32[]{:S(2)}) async-start(bf16[8,48,128]{2,1,0:T(8,128)(2,1)} %ask.1), calls=%async_computation | async-start | bytes 196608 | tf_op jit(solution)/shard_map/all_to_all | solution.py:339
  10.5 0.8 %constant_dynamic-slice_fusion = bf16[16,2048]{1,0:T(8,128)(2,1)S(1)} fusion(bf16[16,4096]{1,0:T(8,128)(2,1)} %param.16, s32[]{:T(128)S(6)} %select_n.7), kind=kLoop, calls=%fused_computation.3 | loop fusion | bytes 131076 | tf_op jit(solution)/shard_map/dynamic_slice | solution.py:306
  11.3 0.0 copy-done
  11.4 0.2 reshape.23
  11.5 0.1 copy.16
  11.7 0.1 reshape.24
  11.8 0.1 reshape.21
  11.9 0.1 copy.15
  12.0 0.0 copy-start.2
  12.1 5.5 %all-to-all-done.asks_ref = bf16[8,48,128]{2,1,0:T(8,128)(2,1)S(1)} async-done(((bf16[8,48,128]{2,1,0:T(8,128)(2,1)}), bf16[8,48,128]{2,1,0:T(8,128)(2,1)S(1)}, u32[]{:S(2)}, u32[]{:S(2)}) %all-to-all-start) | async-done | bytes 98336 | tf_op jit(solution)/shard_map/all_to_all | solution.py:339
  17.6 1.8 %answer.1 = bf16[8,336,128]{2,1,0:T(8,128)(2,1)} custom-call(bf16[8,48,128]{2,1,0:T(8,128)(2,1)S(1)} %all-to-all-done.asks_ref, bf16[16,144,128]{2,1,0:T(8,128)(2,1)S(1)} %pad_maximum_fusion.pool_ref), custom_call_target="tpu_custom_call" | custom-call | tf_op jit(solution)/shard_map/answer/pallas_call | solution.py:340
  19.4 3.6 %all-to-all-start.1 = ((bf16[8,336,128]{2,1,0:T(8,128)(2,1)}), bf16[8,336,128]{2,1,0:T(8,128)(2,1)S(1)}, u32[]{:S(2)}, u32[]{:S(2)}) async-start(bf16[8,336,128]{2,1,0:T(8,128)(2,1)} %answer.1), calls=%async_computation.1 | async-start | bytes 1376256 | tf_op jit(solution)/shard_map/all_to_all | solution.py:356
  23.0 0.0 copy-done.2
  23.0 0.3 copy.18
  23.3 1.4 %copy.19 = bf16[128,32,64]{2,0,1:T(8,128)(2,1)} copy(bf16[128,32,64]{0,2,1:T(8,128)(2,1)S(1)} %bitcast.14) | data formatting | bytes 1048576 | tf_op jit(solution)/shard_map/reshape | solution.py:392
  24.6 6.5 %copy.21 = bf16[128,32,512]{2,0,1:T(8,128)(2,1)} copy(bf16[128,32,512]{2,1,0:T(8,128)(2,1)} %param.11) | data formatting | bytes 8388608 | tf_op args[0]
  31.1 0.0 copy-start.3
  31.1 0.0 copy-start.1
  31.1 5.8 %suffix.1.tail_ref = f32[32,128,128]{2,1,0:T(8,128)} custom-call(bf16[128,512]{1,0:T(8,128)(2,1)} %new_lat_ref.1, bf16[64,128]{1,0:T(8,128)(2,1)} %bitcast.19, bf16[32,128,512]{2,1,0:T(8,128)(2,1)} %bitcast.10, bf16[32,128,64]{2,1,0:T(8,128)(2,1)} %bitcast.12), custom_call_target="tpu_custom_call" | custom-call | flops 603979776 | bytes 12582912 | tf_op jit(solution)/shard_map/suffix/pallas_call | solution.py:394
  36.9 3.0 %all-to-all-done.1.own_ref = bf16[8,336,128]{2,1,0:T(8,128)(2,1)S(1)} async-done(((bf16[8,336,128]{2,1,0:T(8,128)(2,1)}), bf16[8,336,128]{2,1,0:T(8,128)(2,1)S(1)}, u32[]{:S(2)}, u32[]{:S(2)}) %all-to-all-start.1) | async-done | bytes 688160 | tf_op jit(solution)/shard_map/all_to_all | solution.py:356
  39.9 0.0 collective-permute-start
  39.9 0.0 copy-done.3
  39.9 0.1 pad_add_fusion.numbers
  40.0 2.1 %collective-permute-done.sib_ref = bf16[8,336,128]{2,1,0:T(8,128)(2,1)S(1)} collective-permute-done((bf16[8,336,128]{2,1,0:T(8,128)(2,1)S(1)}, bf16[8,336,128]{2,1,0:T(8,128)(2,1)S(1)}, u32[]{:S(2)}, u32[]{:S(2)}) %collective-permute-start) | collective-permute-done | bytes 688160 | tf_op jit(solution)/shard_map/ppermute | solution.py:413
  42.1 0.0 copy-done.1
  42.1 10.4 %attend.1 = (bf16[128,4096]{1,0:T(8,128)(2,1)}, bf16[2,64,512]{2,1,0:T(8,128)(2,1)}, bf16[2,4096]{1,0:T(2,128)(2,1)}) custom-call(s32[7]{0:T(128)S(1)} %pad_add_fusion.numbers, bf16[8,336,128]{2,1,0:T(8,128)(2,1)S(1)} %all-to-all-done.1.own_ref, bf16[8,336,128]{2,1,0:T(8,128)(2,1)S(1)} %collective-permute-done.sib_ref, bf16[128,512]{1,0:T(8,128)(2,1)S(1)} %copy-done.1, ...), custom_call_target="tpu_custom_call" | custom-call | flops 5100273664 | bytes 10485760 | tf_op jit(solution)/shard_map/attend/pallas_call | solution.py:448
  (2 shorter events, 0.1 us)
Async XLA Ops:
  0.6 10.7 %copy-start = (bf16[16,64,512]{2,1,0:T(8,128)(2,1)S(1)}, bf16[16,64,512]{2,1,0:T(8,128)(2,1)}, u32[]{:S(2)}) copy-start(bf16[16,64,512]{2,1,0:T(8,128)(2,1)} %param.15) | copy-start | bytes 3145732
  3.2 14.4 %all-to-all-start = ((bf16[8,48,128]{2,1,0:T(8,128)(2,1)}), bf16[8,48,128]{2,1,0:T(8,128)(2,1)S(1)}, u32[]{:S(2)}, u32[]{:S(2)}) async-start(bf16[8,48,128]{2,1,0:T(8,128)(2,1)} %ask.1), calls=%async_computation | async-start | bytes 196608 | tf_op jit(solution)/shard_map/all_to_all | solution.py:339
  12.0 11.0 %copy-start.2 = (bf16[128,2048]{1,0:T(8,128)(2,1)S(1)}, bf16[128,2048]{1,0:T(8,128)(2,1)}, u32[]{:S(2)}) copy-start(bf16[128,2048]{1,0:T(8,128)(2,1)} %param.12) | copy-start | bytes 1572868
  19.4 20.5 %all-to-all-start.1 = ((bf16[8,336,128]{2,1,0:T(8,128)(2,1)}), bf16[8,336,128]{2,1,0:T(8,128)(2,1)S(1)}, u32[]{:S(2)}, u32[]{:S(2)}) async-start(bf16[8,336,128]{2,1,0:T(8,128)(2,1)} %answer.1), calls=%async_computation.1 | async-start | bytes 1376256 | tf_op jit(solution)/shard_map/all_to_all | solution.py:356
  31.1 8.8 %copy-start.3 = (s32[6,1]{0,1:T(1,128)S(1)}, s32[6,1]{0,1:T(1,128)}, u32[]{:S(2)}) copy-start(s32[6,1]{0,1:T(1,128)} %param.18) | copy-start | bytes 76
  31.1 10.9 %copy-start.1 = (bf16[128,512]{1,0:T(8,128)(2,1)S(1)}, bf16[128,512]{1,0:T(8,128)(2,1)}, u32[]{:S(2)}) copy-start(bf16[128,512]{1,0:T(8,128)(2,1)} %new_lat_ref.1) | copy-start | bytes 393220
  39.9 2.1 %collective-permute-start = (bf16[8,336,128]{2,1,0:T(8,128)(2,1)S(1)}, bf16[8,336,128]{2,1,0:T(8,128)(2,1)S(1)}, u32[]{:S(2)}, u32[]{:S(2)}) collective-permute-start(bf16[8,336,128]{2,1,0:T(8,128)(2,1)S(1)} %all-to-all-done.1.own_ref), channel_id=1, source_target_pairs={{0,1},{1,0},{2,3},{3,2},{4,5},{5,4},{6,7},{7,6},{8,9},{9,8},{10,11... | collective-permute-start | bytes 2064392 | tf_op jit(solution)/shard_map/ppermute | solution.py:413

commit v5 on v4

--- a/solution.py
+++ b/solution.py
@@ -63,8 +63,9 @@
         ask = jnp.where(lane == 2 * hits + s, new_place[s], ask)
     ask = ask.astype(jnp.float32)
 
-    token_keep = lax.broadcasted_iota(jnp.int32, tokens.shape, 0) < length[0]
-    tokens[...] = jnp.where(token_keep, rope_ref[...].astype(jnp.float32).T, 0.0)
+    turned = rope_ref[...].astype(jnp.float32).T
+    token_keep = lax.broadcasted_iota(jnp.int32, turned.shape, 0) < length[0]
+    tokens[: turned.shape[0], :] = jnp.where(token_keep, turned, 0.0)
     for b in range(new_count):
         base = b * block_len + core * half
         at = pl.multiple_of(base, half)
@@ -91,7 +92,7 @@
         out_ref[j, new_count * part :, :] = rows32[j].astype(out_ref.dtype)
 
 
-def answer_kernel(hits, new_count, asks_ref, pool_ref, out_ref, rows32, ids_vec, ids, sem):
+def answer_kernel(hits, new_count, asks_ref, pool_ref, out_any, out_ref, rows32, ids_vec, ids, sem, out_sems):
     me = lax.axis_index("pool")
     peers, depth = out_ref.shape[0], pool_ref.shape[1]
     tail = asks_ref.shape[1] - 16
@@ -133,9 +134,15 @@
             merged = jnp.where(pairs_row % new_count == s, shifted, merged)
         both = jnp.concatenate([merged, jnp.zeros((8, LANES), jnp.float32)], axis=0)
         out_ref[r, base + tail :, :] = both.astype(out_ref.dtype)
+        leave(r).start()
         return carry
 
+    def leave(r):
+        return pltpu.make_async_copy(out_ref.at[r], out_any.at[r], out_sems.at[r])
+
     lax.fori_loop(0, peers, body, 0)
+    for r in range(peers):
+        leave(r).wait()
 
 
 def write_back(block_len, base, own_ref, sib_ref, lat_ref, rope_ref):
@@ -328,7 +335,7 @@
                 pltpu.SMEM(new_place.shape, jnp.int32),
                 pltpu.VMEM((rows, latent), new_lat.dtype),
                 pltpu.VMEM((rope_width, rows), new_rope.dtype),
-                pltpu.VMEM((rows, rope_width), jnp.float32),
+                pltpu.VMEM((rows + 8, rope_width), jnp.float32),
                 pltpu.VMEM((peers, 16, LANES), jnp.float32),
                 pltpu.SemaphoreType.DMA((6,)),
             ],
@@ -340,12 +347,14 @@
         found = pl.pallas_call(
             functools.partial(answer_kernel, hits, new_count),
             in_specs=[whole] * 2,
-            out_specs=whole,
+            out_specs=anywhere,
             scratch_shapes=[
+                pltpu.VMEM((peers, CAP * depth + new_count * part + 16, LANES), cached.dtype),
                 pltpu.VMEM((peers, 16, LANES), jnp.float32),
                 pltpu.VMEM((peers, LANES), jnp.int32),
                 pltpu.SMEM((peers, LANES), jnp.int32),
                 pltpu.SemaphoreType.DMA,
+                pltpu.SemaphoreType.DMA((peers,)),
             ],
             out_shape=jax.ShapeDtypeStruct(
                 (peers, CAP * depth + new_count * part + 16, LANES), cached.dtype

time: 53 us -> 52.9 us (level)
  transfers between devices with their start and end apart: 3 -> 3, of which waited for: 3 -> 3; matrix products, arithmetic and copies ran while one was open for 18% -> 19% of each run, Pallas kernels for 11% -> 11%
where the time goes in v5:
time: 52.9 us; the launch traced here: 52.4 us
  Pallas kernels  19.7 us (37%)
  starting transfers between devices  10.9 us (21%)
  waiting for transfers between devices  10.6 us (20%)
  local copies, waits for them, and re-layouts  9.61 us (18%)
  between operations  1.49 us (3%)
    pallas_call x1, Pallas kernels, local(): pl.pallas_call(functools.partial(attend_kernel, block_len, hits), grid_sp...  10.4 us
    all_to_all x1, starting transfers between devices, local(): lax.all_to_all(asked, 'pool', split_axis=0, concat_axis=0, tiled=True)  7.29 us
    unnamed x10, local copies, waits for them, and re-layouts  6.76 us
    pallas_call x1, Pallas kernels, local(): pl.pallas_call(functools.partial(suffix_kernel, group), in_specs=[whole]...  5.78 us
    all_to_all x1, waiting for transfers between devices, local(): lax.all_to_all(asked, 'pool', split_axis=0, concat_axis=0, tiled=True)  5.52 us
    all_to_all x1, starting transfers between devices, local(): own = lax.all_to_all(found, 'pool', split_axis=0, concat_axis=0, tiled=True)  3.56 us
    all_to_all x1, waiting for transfers between devices, local(): own = lax.all_to_all(found, 'pool', split_axis=0, concat_axis=0, tiled=True)  3.01 us
    ppermute x1, waiting for transfers between devices, local(): sib = lax.ppermute(own, 'tp', swap)  2.06 us
  transfers between devices with their start and end apart: 3, of which 3 were waited for; matrix products, arithmetic and copies ran while one was open for 19% of the time, Pallas kernels for 11%

profile of v5, /device:TPU:0, one launch (start us, length us, event | category | flops | bytes accessed | tf_op | source)
XLA Modules:
  0.0 52.4 jit_solution(17625072296261442596)
XLA Ops:
  0.6 0.0 copy-start
  1.4 1.8 %ask.1 = bf16[8,48,128]{2,1,0:T(8,128)(2,1)} custom-call(s32[6]{0:T(128)} %refs_0_.1, s32[6]{0:T(128)} %bitcast.20, s32[1]{0:T(128)S(6)} %copy.22.refs_2_, s32[2]{0:T(128)} %refs_3_.1, bf16[128,512]{1,0:T(8,128)(2,1)} %new_lat_ref.1, bf16[64,128]{1,0:T(8,128)(2,1)} %bitcast.18), custom_call_target="tpu_custom_call" | custom-call | tf_op jit(solution)/shard_map/ask/pallas_call | solution.py:327
  3.2 7.3 %all-to-all-start = ((bf16[8,48,128]{2,1,0:T(8,128)(2,1)}), bf16[8,48,128]{2,1,0:T(8,128)(2,1)S(1)}, u32[]{:S(2)}, u32[]{:S(2)}) async-start(bf16[8,48,128]{2,1,0:T(8,128)(2,1)} %ask.1), calls=%async_computation | async-start | bytes 196608 | tf_op jit(solution)/shard_map/all_to_all | solution.py:346
  10.5 0.8 %constant_dynamic-slice_fusion = bf16[16,2048]{1,0:T(8,128)(2,1)S(1)} fusion(bf16[16,4096]{1,0:T(8,128)(2,1)} %param.16, s32[]{:T(128)S(6)} %select_n.7), kind=kLoop, calls=%fused_computation.3 | loop fusion | bytes 131076 | tf_op jit(solution)/shard_map/dynamic_slice | solution.py:313
  11.3 0.0 copy-done
  11.4 0.2 reshape.23
  11.5 0.1 copy.16
  11.7 0.1 reshape.24
  11.8 0.1 reshape.21
  11.9 0.1 copy.15
  12.0 0.0 copy-start.2
  12.1 5.5 %all-to-all-done.asks_ref = bf16[8,48,128]{2,1,0:T(8,128)(2,1)S(1)} async-done(((bf16[8,48,128]{2,1,0:T(8,128)(2,1)}), bf16[8,48,128]{2,1,0:T(8,128)(2,1)S(1)}, u32[]{:S(2)}, u32[]{:S(2)}) %all-to-all-start) | async-done | bytes 98336 | tf_op jit(solution)/shard_map/all_to_all | solution.py:346
  17.6 1.7 %answer.1 = bf16[8,336,128]{2,1,0:T(8,128)(2,1)} custom-call(bf16[8,48,128]{2,1,0:T(8,128)(2,1)S(1)} %all-to-all-done.asks_ref, bf16[16,144,128]{2,1,0:T(8,128)(2,1)S(1)} %pad_maximum_fusion.pool_ref), custom_call_target="tpu_custom_call" | custom-call | tf_op jit(solution)/shard_map/answer/pallas_call | solution.py:347
  19.3 3.6 %all-to-all-start.1 = ((bf16[8,336,128]{2,1,0:T(8,128)(2,1)}), bf16[8,336,128]{2,1,0:T(8,128)(2,1)S(1)}, u32[]{:S(2)}, u32[]{:S(2)}) async-start(bf16[8,336,128]{2,1,0:T(8,128)(2,1)} %answer.1), calls=%async_computation.1 | async-start | bytes 1376256 | tf_op jit(solution)/shard_map/all_to_all | solution.py:365
  22.9 0.0 copy-done.2
  22.9 0.3 copy.18
  23.2 1.4 %copy.19 = bf16[128,32,64]{2,0,1:T(8,128)(2,1)} copy(bf16[128,32,64]{0,2,1:T(8,128)(2,1)S(1)} %bitcast.14) | data formatting | bytes 1048576 | tf_op jit(solution)/shard_map/reshape | solution.py:401
  24.5 6.5 %copy.21 = bf16[128,32,512]{2,0,1:T(8,128)(2,1)} copy(bf16[128,32,512]{2,1,0:T(8,128)(2,1)} %param.11) | data formatting | bytes 8388608 | tf_op args[0]
  31.0 0.0 copy-start.3
  31.0 0.0 copy-start.1
  31.0 5.8 %suffix.1.tail_ref = f32[32,128,128]{2,1,0:T(8,128)} custom-call(bf16[128,512]{1,0:T(8,128)(2,1)} %new_lat_ref.1, bf16[64,128]{1,0:T(8,128)(2,1)} %bitcast.19, bf16[32,128,512]{2,1,0:T(8,128)(2,1)} %bitcast.10, bf16[32,128,64]{2,1,0:T(8,128)(2,1)} %bitcast.12), custom_call_target="tpu_custom_call" | custom-call | flops 603979776 | bytes 12582912 | tf_op jit(solution)/shard_map/suffix/pallas_call | solution.py:403
  36.8 3.0 %all-to-all-done.1.own_ref = bf16[8,336,128]{2,1,0:T(8,128)(2,1)S(1)} async-done(((bf16[8,336,128]{2,1,0:T(8,128)(2,1)}), bf16[8,336,128]{2,1,0:T(8,128)(2,1)S(1)}, u32[]{:S(2)}, u32[]{:S(2)}) %all-to-all-start.1) | async-done | bytes 688160 | tf_op jit(solution)/shard_map/all_to_all | solution.py:365
  39.8 0.0 collective-permute-start
  39.8 0.0 copy-done.3
  39.8 0.1 pad_add_fusion.numbers
  39.9 2.1 %collective-permute-done.sib_ref = bf16[8,336,128]{2,1,0:T(8,128)(2,1)S(1)} collective-permute-done((bf16[8,336,128]{2,1,0:T(8,128)(2,1)S(1)}, bf16[8,336,128]{2,1,0:T(8,128)(2,1)S(1)}, u32[]{:S(2)}, u32[]{:S(2)}) %collective-permute-start) | collective-permute-done | bytes 688160 | tf_op jit(solution)/shard_map/ppermute | solution.py:422
  41.9 0.0 copy-done.1
  41.9 10.4 %attend.1 = (bf16[128,4096]{1,0:T(8,128)(2,1)}, bf16[2,64,512]{2,1,0:T(8,128)(2,1)}, bf16[2,4096]{1,0:T(2,128)(2,1)}) custom-call(s32[7]{0:T(128)S(1)} %pad_add_fusion.numbers, bf16[8,336,128]{2,1,0:T(8,128)(2,1)S(1)} %all-to-all-done.1.own_ref, bf16[8,336,128]{2,1,0:T(8,128)(2,1)S(1)} %collective-permute-done.sib_ref, bf16[128,512]{1,0:T(8,128)(2,1)S(1)} %copy-done.1, ...), custom_call_target="tpu_custom_call" | custom-call | flops 5100273664 | bytes 10485760 | tf_op jit(solution)/shard_map/attend/pallas_call | solution.py:457
  (2 shorter events, 0.1 us)
Async XLA Ops:
  0.6 10.7 %copy-start = (bf16[16,64,512]{2,1,0:T(8,128)(2,1)S(1)}, bf16[16,64,512]{2,1,0:T(8,128)(2,1)}, u32[]{:S(2)}) copy-start(bf16[16,64,512]{2,1,0:T(8,128)(2,1)} %param.15) | copy-start | bytes 3145732
  3.2 14.4 %all-to-all-start = ((bf16[8,48,128]{2,1,0:T(8,128)(2,1)}), bf16[8,48,128]{2,1,0:T(8,128)(2,1)S(1)}, u32[]{:S(2)}, u32[]{:S(2)}) async-start(bf16[8,48,128]{2,1,0:T(8,128)(2,1)} %ask.1), calls=%async_computation | async-start | bytes 196608 | tf_op jit(solution)/shard_map/all_to_all | solution.py:346
  12.0 10.9 %copy-start.2 = (bf16[128,2048]{1,0:T(8,128)(2,1)S(1)}, bf16[128,2048]{1,0:T(8,128)(2,1)}, u32[]{:S(2)}) copy-start(bf16[128,2048]{1,0:T(8,128)(2,1)} %param.12) | copy-start | bytes 1572868
  19.3 20.5 %all-to-all-start.1 = ((bf16[8,336,128]{2,1,0:T(8,128)(2,1)}), bf16[8,336,128]{2,1,0:T(8,128)(2,1)S(1)}, u32[]{:S(2)}, u32[]{:S(2)}) async-start(bf16[8,336,128]{2,1,0:T(8,128)(2,1)} %answer.1), calls=%async_computation.1 | async-start | bytes 1376256 | tf_op jit(solution)/shard_map/all_to_all | solution.py:365
  31.0 8.8 %copy-start.3 = (s32[6,1]{0,1:T(1,128)S(1)}, s32[6,1]{0,1:T(1,128)}, u32[]{:S(2)}) copy-start(s32[6,1]{0,1:T(1,128)} %param.18) | copy-start | bytes 76
  31.0 10.9 %copy-start.1 = (bf16[128,512]{1,0:T(8,128)(2,1)S(1)}, bf16[128,512]{1,0:T(8,128)(2,1)}, u32[]{:S(2)}) copy-start(bf16[128,512]{1,0:T(8,128)(2,1)} %new_lat_ref.1) | copy-start | bytes 393220
  39.8 2.1 %collective-permute-start = (bf16[8,336,128]{2,1,0:T(8,128)(2,1)S(1)}, bf16[8,336,128]{2,1,0:T(8,128)(2,1)S(1)}, u32[]{:S(2)}, u32[]{:S(2)}) collective-permute-start(bf16[8,336,128]{2,1,0:T(8,128)(2,1)S(1)} %all-to-all-done.1.own_ref), channel_id=1, source_target_pairs={{0,1},{1,0},{2,3},{3,2},{4,5},{5,4},{6,7},{7,6},{8,9},{9,8},{10,11... | collective-permute-start | bytes 2064392 | tf_op jit(solution)/shard_map/ppermute | solution.py:422
